TPU v7x, 32 devices: a whole 2x2x4 slice. The times are simulated.
32 devices in a mesh: ep: 4 (over y, x), tp: 8 (over z, core).
Axes of the slice: x: 2, y: 2, z: 4, core: 2. Of those that a mesh axis runs over, the one named last changes fastest.
Arguments:
- tokens: bfloat16 [256, 7168], P(('ep', 'tp')), may hold values from -6 to 6
- cotangent: bfloat16 [256, 7168], P(('ep', 'tp')), may hold values from -6 to 6
- routing: int32 [256, 2], P(('ep', 'tp')), may hold values from 0 to 7, all different within a row; in each aligned block of 8 rows (0 to 7, 8 to 15, ...) at most 3 rows name the same one
- route_gates: bfloat16 [256, 2], P(('ep', 'tp')), may hold values from 0.5 to 2.5
- gate_weight: bfloat16 [8, 2048, 7168], P(None, 'tp', 'ep'), may hold values from -0.0625 to 0.0625
- up_weight: bfloat16 [8, 2048, 7168], P(None, 'tp', 'ep'), may hold values from -0.0625 to 0.0625
- down_weight: bfloat16 [8, 2048, 7168], P(None, 'tp', 'ep'), may hold values from -0.125 to 0.125
Outputs:
- token_grad: bfloat16 [256, 7168], P(('ep', 'tp'))
- route_grad: float32 [256, 2], P(('ep', 'tp'))
- gate_grad: bfloat16 [8, 2048, 7168], P(None, 'tp', 'ep')
- up_grad: bfloat16 [8, 2048, 7168], P(None, 'tp', 'ep')
- down_grad: bfloat16 [8, 2048, 7168], P(None, 'tp', 'ep')
Inputs may be any that keep to these rules, and one draw needn't show every extreme that they name: `routing`: in the rows of one device a row names 2 different experts, no expert is named more than 3 times, a bound that some block reaches.
All inputs are finite; a program needn't handle non-finite values.
Results may differ from a plain program's by a relative error of at most 0.017.
Values may be sent and summed in bfloat16 or wider, within the bound.
A program may use at most 192 MiB of HBM per device.

v0:
```python
import jax
import jax.numpy as jnp
from jax import lax
from jax.sharding import PartitionSpec as P

MOST = 3


def gather_rows(local_x, local_dy, local_p):
    return (
        lax.all_gather(local_x, "tp", axis=1, tiled=True),
        lax.all_gather(local_dy, "tp", axis=1, tiled=True),
        lax.all_gather(local_p, "tp", axis=1, tiled=True),
    )


def expert_terms(rows_x, rows_dy, rows_p, gate_mat, up_mat, down_mat, finish):
    gate_pre = jnp.einsum("erd,ehd->erh", rows_x, gate_mat, preferred_element_type=jnp.float32)
    upper_pre = jnp.einsum("erd,ehd->erh", rows_x, up_mat, preferred_element_type=jnp.float32)
    down_pre = jnp.einsum("erd,ehd->erh", rows_dy, down_mat, preferred_element_type=jnp.float32)
    gate, upper, reverse = finish(gate_pre, upper_pre, down_pre)
    hidden = (jax.nn.silu(gate) * upper).astype(jnp.bfloat16)
    factor = rows_p.astype(jnp.float32)[:, :, None]
    back = factor * reverse
    route_part = jnp.sum(hidden.astype(jnp.float32) * reverse, axis=2)
    sigma = jax.nn.sigmoid(gate)
    d_gate = (back * upper * sigma * (1.0 + gate * (1.0 - sigma))).astype(jnp.bfloat16)
    d_up = (back * jax.nn.silu(gate)).astype(jnp.bfloat16)
    input_part = jnp.einsum("erh,ehd->erd", d_gate, gate_mat, preferred_element_type=jnp.float32)
    input_part = input_part + jnp.einsum(
        "erh,ehd->erd", d_up, up_mat, preferred_element_type=jnp.float32
    )
    grad_gate = jnp.einsum(
        "erh,erd->ehd", d_gate, rows_x, preferred_element_type=jnp.float32
    ).astype(jnp.bfloat16)
    grad_up = jnp.einsum("erh,erd->ehd", d_up, rows_x, preferred_element_type=jnp.float32).astype(
        jnp.bfloat16
    )
    scaled = (factor * hidden.astype(jnp.float32)).astype(jnp.bfloat16)
    grad_down = jnp.einsum(
        "erh,erd->ehd", scaled, rows_dy, preferred_element_type=jnp.float32
    ).astype(jnp.bfloat16)
    slot_sums = lax.psum_scatter(
        input_part.astype(jnp.bfloat16), "tp", scatter_dimension=1, tiled=True
    ).astype(jnp.float32)
    return (slot_sums, route_part, grad_gate, grad_up, grad_down)


def keep_sums(gate_pre, upper_pre, down_pre):
    return (gate_pre, upper_pre, down_pre)


def local(tokens, cotangent, routing, route_gates, gate_weight, up_weight, down_weight):
    tok_rows, width = tokens.shape
    top_count = routing.shape[1]
    experts = gate_weight.shape[0]
    entries = tok_rows * top_count
    flat_route = routing.reshape(entries)
    expert_iota = jnp.arange(experts, dtype=jnp.int32)
    onehot = (flat_route[:, None] == expert_iota[None, :]).astype(jnp.int32)
    before = jnp.cumsum(onehot, axis=0) - onehot
    slot_rank = jnp.sum(before * onehot, axis=1)
    target = flat_route * MOST + slot_rank
    slot_iota = jnp.arange(experts * MOST, dtype=jnp.int32)
    select = (target[None, :] == slot_iota[:, None]).astype(jnp.float32)
    placing = jnp.sum(select.reshape(experts * MOST, tok_rows, top_count), axis=2)
    placing_low = placing.astype(jnp.bfloat16)
    send_x = (
        jnp.dot(placing_low, tokens, preferred_element_type=jnp.float32)
        .astype(jnp.bfloat16)
        .reshape(experts, MOST, width)
    )
    send_dy = (
        jnp.dot(placing_low, cotangent, preferred_element_type=jnp.float32)
        .astype(jnp.bfloat16)
        .reshape(experts, MOST, width)
    )
    gate_flat = route_gates.reshape(entries).astype(jnp.float32)
    send_p = (
        jnp.dot(select, gate_flat, precision=lax.Precision.HIGHEST)
        .astype(jnp.bfloat16)
        .reshape(experts, MOST)
    )
    new_gate, new_up, new_down = (
        lax.all_to_all(gate_weight, "ep", split_axis=0, concat_axis=2, tiled=True),
        lax.all_to_all(up_weight, "ep", split_axis=0, concat_axis=2, tiled=True),
        lax.all_to_all(down_weight, "ep", split_axis=0, concat_axis=2, tiled=True),
    )
    local_x, local_dy, local_p = (
        lax.all_to_all(send_x, "ep", split_axis=0, concat_axis=1, tiled=True),
        lax.all_to_all(send_dy, "ep", split_axis=0, concat_axis=1, tiled=True),
        lax.all_to_all(send_p, "ep", split_axis=0, concat_axis=1, tiled=True),
    )
    rows_x, rows_dy, rows_p = gather_rows(local_x, local_dy, local_p)
    slot_sums, route_part, grad_gate, grad_up, grad_down = expert_terms(
        rows_x, rows_dy, rows_p, new_gate, new_up, new_down, keep_sums
    )
    route_sums = lax.psum_scatter(route_part, "tp", scatter_dimension=1, tiled=True)
    back_x, back_route = (
        lax.all_to_all(
            slot_sums.astype(jnp.bfloat16), "ep", split_axis=1, concat_axis=0, tiled=True
        ).astype(slot_sums.dtype),
        lax.all_to_all(
            route_sums.astype(jnp.bfloat16), "ep", split_axis=1, concat_axis=0, tiled=True
        ).astype(route_sums.dtype),
    )
    gate_grad, up_grad, down_grad = (
        lax.all_to_all(grad_gate, "ep", split_axis=2, concat_axis=0, tiled=True),
        lax.all_to_all(grad_up, "ep", split_axis=2, concat_axis=0, tiled=True),
        lax.all_to_all(grad_down, "ep", split_axis=2, concat_axis=0, tiled=True),
    )
    slot_flat = back_x.reshape(experts * MOST, width)
    token_grad = jnp.dot(
        placing.T, slot_flat, precision=lax.Precision.HIGHEST, preferred_element_type=jnp.float32
    ).astype(jnp.bfloat16)
    route_flat = back_route.reshape(experts * MOST)
    route_grad = jnp.dot(select.T, route_flat, precision=lax.Precision.HIGHEST).reshape(
        tok_rows, top_count
    )
    return (token_grad, route_grad, gate_grad, up_grad, down_grad)


def solution(mesh):
    placed = (
        P(("ep", "tp"), None),
        P(("ep", "tp"), None),
        P(("ep", "tp"), None),
        P(("ep", "tp"), None),
        P(None, "tp", "ep"),
        P(None, "tp", "ep"),
        P(None, "tp", "ep"),
    )
    return jax.shard_map(
        local,
        mesh=mesh,
        in_specs=placed,
        out_specs=(
            P(("ep", "tp"), None),
            P(("ep", "tp"), None),
            P(None, "tp", "ep"),
            P(None, "tp", "ep"),
            P(None, "tp", "ep"),
        ),
        check_vma=False,
    )
```

profile of v0, /device:TPU:0, one launch (start us, length us, event | category | flops | bytes accessed | tf_op | source)
XLA Modules:
  0.0 726.8 jit_solution(14975879346308514302)
XLA Ops:
  7.2 0.8 copy.100
  8.0 0.1 reshape.88
  8.1 0.8 copy.97
  9.0 0.2 select_reduce_fusion
  9.2 0.1 fusion.10
  9.3 0.7 all_to_all.141
  10.0 5.2 all-to-all-start
  15.3 0.6 copy-done.9
  16.0 0.3 convolution_convert_fusion.3
  16.3 1.0 reshape.82
  17.3 2.5 all-to-all-done
  19.7 3.5 all-to-all-start.3
  23.2 1.2 convolution_convert_fusion.4
  24.4 0.2 reshape.81
  24.6 4.8 all-to-all-done.3
  29.4 9.5 %all_to_all.194 = bf16[8,3,7168]{2,1,0:T(4,128)(2,1)S(1)} all-to-all(bf16[8,3,7168]{2,1,0:T(4,128)(2,1)S(1)} %reshape.81), channel_id=1, replica_groups=mesh['ep'=4,'tp'=8] {'ep'}, dimensions={0} | all-to-all | bytes 688128 | tf_op jit(solution)/shard_map/all_to_all | solution.py:91
  38.9 85.4 %all_to_all.195 = bf16[8,256,1792]{2,1,0:T(8,128)(2,1)} all-to-all(bf16[8,256,1792]{2,1,0:T(8,128)(2,1)} %param.11), channel_id=1, replica_groups=mesh['ep'=4,'tp'=8] {'ep'}, dimensions={0} | all-to-all | bytes 14680064 | tf_op jit(solution)/shard_map/all_to_all | solution.py:85
  124.3 5.5 all-to-all-start.4
  129.8 1.0 copy.106
  130.9 75.3 %all-to-all-done.4 = bf16[8,256,1792]{2,1,0:T(8,128)(2,1)} async-done(((bf16[8,256,1792]{2,1,0:T(8,128)(2,1)}), bf16[8,256,1792]{2,1,0:T(8,128)(2,1)}, u32[]{:S(2)}, u32[]{:S(2)}) %all-to-all-start.4) | async-done | bytes 7340064 | tf_op jit(solution)/shard_map/all_to_all | solution.py:86
  206.2 5.4 all-to-all-start.2
  211.7 1.0 copy.103
  212.9 11.9 %all-gather = bf16[8,12,2]{1,2,0:T(2,128)(2,1)S(1)} all-gather(bf16[1,12,2]{1,2,0:T(2,128)(2,1)S(1)} %bitcast.91), channel_id=1, replica_groups=mesh['ep'=4,'tp'=8] {'tp'}, dimensions={0}, use_global_device_ids=true | all-gather | bytes 432 | tf_op jit(solution)/shard_map/all_gather | solution.py:13
  224.9 11.8 %copy.145 = bf16[4,2,256,1792]{3,0,2,1:T(4,128)(2,1)} copy(bf16[4,2,256,1792]{3,2,1,0:T(8,128)(2,1)} %bitcast.75) | data formatting | bytes 14680064 | tf_op jit(solution)/shard_map/all_to_all | solution.py:85
  236.7 13.5 %all_to_all.164 = bf16[2,256,7168]{2,1,0:T(8,128)(2,1)} reshape(bf16[2,256,4,1792]{3,2,1,0:T(4,128)(2,1)} %bitcast.76) | data formatting | bytes 14680064 | tf_op jit(solution)/shard_map/all_to_all | solution.py:85
  250.2 11.8 %copy.146 = bf16[4,2,256,1792]{3,0,2,1:T(4,128)(2,1)} copy(bf16[4,2,256,1792]{3,2,1,0:T(8,128)(2,1)} %bitcast.13) | data formatting | bytes 14680064 | tf_op jit(solution)/shard_map/all_to_all | solution.py:86
  262.0 13.5 %all_to_all.160 = bf16[2,256,7168]{2,1,0:T(8,128)(2,1)} reshape(bf16[2,256,4,1792]{3,2,1,0:T(4,128)(2,1)} %bitcast.77) | data formatting | bytes 14680064 | tf_op jit(solution)/shard_map/all_to_all | solution.py:86
  275.5 16.7 %all-to-all-done.2 = bf16[8,256,1792]{2,1,0:T(8,128)(2,1)} async-done(((bf16[8,256,1792]{2,1,0:T(8,128)(2,1)}), bf16[8,256,1792]{2,1,0:T(8,128)(2,1)}, u32[]{:S(2)}, u32[]{:S(2)}) %all-to-all-start.2) | async-done | bytes 7340064 | tf_op jit(solution)/shard_map/all_to_all | solution.py:87
  292.2 11.8 %copy.147 = bf16[4,2,256,1792]{3,0,2,1:T(4,128)(2,1)} copy(bf16[4,2,256,1792]{3,2,1,0:T(8,128)(2,1)} %bitcast.8) | data formatting | bytes 14680064 | tf_op jit(solution)/shard_map/all_to_all | solution.py:87
  304.0 13.6 %all_to_all.152 = bf16[2,256,7168]{2,1,0:T(8,128)(2,1)} reshape(bf16[2,256,4,1792]{3,2,1,0:T(4,128)(2,1)} %bitcast.78) | data formatting | bytes 14680064 | tf_op jit(solution)/shard_map/all_to_all | solution.py:87
  317.6 6.5 fusion.6
  324.0 0.3 copy-done.3
  324.3 3.1 fusion.8
  327.4 7.1 fusion.11
  334.5 1.3 fusion.24
  335.8 0.9 slice-done.3
  336.7 1.3 fusion
  338.0 4.4 copy.111
  342.4 0.6 dynamic-slice
  343.7 16.3 %all-reduce.1 = bf16[2,96]{1,0:T(2,128)(2,1)S(1)} all-reduce(f32[2,96]{1,0:T(2,128)S(1)} %get-tuple-element.5), channel_id=3, replica_groups=mesh['ep'=4,'tp'=8] {'tp'}, use_global_device_ids=true, to_apply=%region_5.6.clone | all-reduce | flops 192 | bytes 1152
  360.1 0.6 copy.114
  360.7 3.2 all-to-all-start.7
  363.9 49.9 %all-reduce.4.cloned.1.call-done = bf16[2,96,7168]{2,0,1:T(2,128)(2,1)} async-done(((bf16[2,96,7168]{2,0,1:T(2,128)(2,1)}), bf16[2,96,7168]{2,0,1:T(2,128)(2,1)}) %all-reduce.4.cloned.1.call-update) | async-done | bytes 2752528
  413.8 1.9 constant_dynamic-slice_fusion
  415.8 3.9 all-to-all-start.6
  419.7 5.3 convolution_convert_fusion
  425.0 18.5 %copy.122 = bf16[2,256,7168]{1,0,2:T(2,128)(2,1)} copy(bf16[2,256,7168]{2,1,0:T(8,128)(2,1)} %convolution_convert_fusion) | data formatting | bytes 14680064 | tf_op jit(solution)/shard_map/convert_element_type | solution.py:42
  443.5 5.7 all-to-all-start.10
  449.3 5.2 convolution_convert_fusion.2
  454.5 18.5 %copy.116 = bf16[2,256,7168]{1,0,2:T(2,128)(2,1)} copy(bf16[2,256,7168]{2,1,0:T(8,128)(2,1)} %convolution_convert_fusion.2) | data formatting | bytes 14680064 | tf_op jit(solution)/shard_map/convert_element_type | solution.py:35
  473.0 56.2 %all-to-all-done.10 = bf16[2,256,7168]{1,0,2:T(2,128)(2,1)} async-done(((bf16[2,256,7168]{1,0,2:T(2,128)(2,1)}), bf16[2,256,7168]{1,0,2:T(2,128)(2,1)}, u32[]{:S(2)}, u32[]{:S(2)}) %all-to-all-start.10) | async-done | bytes 7340064 | tf_op jit(solution)/shard_map/all_to_all | solution.py:110
  529.2 5.5 all-to-all-start.8
  534.7 5.2 convolution_convert_fusion.1
  539.9 18.6 %copy.119 = bf16[2,256,7168]{1,0,2:T(2,128)(2,1)} copy(bf16[2,256,7168]{2,1,0:T(8,128)(2,1)} %convolution_convert_fusion.1) | data formatting | bytes 14680064 | tf_op jit(solution)/shard_map/convert_element_type | solution.py:36
  558.5 56.8 %all-to-all-done.8 = bf16[2,256,7168]{1,0,2:T(2,128)(2,1)} async-done(((bf16[2,256,7168]{1,0,2:T(2,128)(2,1)}), bf16[2,256,7168]{1,0,2:T(2,128)(2,1)}, u32[]{:S(2)}, u32[]{:S(2)}) %all-to-all-start.8) | async-done | bytes 7340064 | tf_op jit(solution)/shard_map/all_to_all | solution.py:108
  615.3 5.4 all-to-all-start.9
  620.8 0.8 fusion.18
  621.6 0.2 copy.112
  621.8 0.3 reshape.83
  622.1 0.9 convolution_convert_fusion.5
  623.0 18.4 %copy.123 = bf16[4,2,256,1792]{3,2,1,0:T(8,128)(2,1)} copy(bf16[4,2,256,1792]{2,1,3,0:T(2,128)(2,1)} %bitcast.29) | data formatting | bytes 14680064 | tf_op jit(solution)/shard_map/all_to_all | solution.py:110
  641.5 18.4 %copy.117 = bf16[4,2,256,1792]{3,2,1,0:T(8,128)(2,1)} copy(bf16[4,2,256,1792]{2,1,3,0:T(2,128)(2,1)} %bitcast.23) | data formatting | bytes 14680064 | tf_op jit(solution)/shard_map/all_to_all | solution.py:108
  659.9 41.4 %all-to-all-done.9 = bf16[2,256,7168]{1,0,2:T(2,128)(2,1)} async-done(((bf16[2,256,7168]{1,0,2:T(2,128)(2,1)}), bf16[2,256,7168]{1,0,2:T(2,128)(2,1)}, u32[]{:S(2)}, u32[]{:S(2)}) %all-to-all-start.9) | async-done | bytes 7340064 | tf_op jit(solution)/shard_map/all_to_all | solution.py:109
  701.3 18.5 %copy.120 = bf16[4,2,256,1792]{3,2,1,0:T(8,128)(2,1)} copy(bf16[4,2,256,1792]{2,1,3,0:T(2,128)(2,1)} %bitcast.26) | data formatting | bytes 14680064 | tf_op jit(solution)/shard_map/all_to_all | solution.py:109
  (56 shorter events, 1.1 us)
Async XLA Ops:
  7.2 8.8 %copy-start = (bf16[8,7168]{1,0:T(8,128)(2,1)S(1)}, bf16[8,7168]{1,0:T(8,128)(2,1)}, u32[]{:S(2)}) copy-start(bf16[8,7168]{1,0:T(8,128)(2,1)} %param.7) | copy-start | bytes 344068
  10.0 9.7 %all-to-all-start = ((bf16[4,2,3]{2,1,0:T(2,128)(2,1)}), bf16[4,2,3]{2,1,0:T(2,128)(2,1)S(1)}, u32[]{:S(2)}, u32[]{:S(2)}) async-start(bf16[4,2,3]{2,1,0:T(2,128)(2,1)} %all_to_all.141), calls=%async_computation | async-start | bytes 4096 | tf_op jit(solution)/shard_map/all_to_all | solution.py:92
  15.3 0.6 copy-start.9
  16.0 8.6 %copy-start.7 = (f32[24,8]{0,1:T(8,128)}, f32[24,8]{0,1:T(8,128)S(1)}, u32[]{:S(2)}) copy-start(f32[24,8]{0,1:T(8,128)S(1)} %convert_reduce_fusion) | copy-start | bytes 2308
  19.7 9.7 %all-to-all-start.3 = ((bf16[8,3,7168]{2,1,0:T(4,128)(2,1)}), bf16[8,3,7168]{2,1,0:T(4,128)(2,1)S(1)}, u32[]{:S(2)}, u32[]{:S(2)}) async-start(bf16[8,3,7168]{2,1,0:T(4,128)(2,1)} %reshape.82), calls=%async_computation.3 | async-start | bytes 917504 | tf_op jit(solution)/shard_map/all_to_all | solution.py:90
  124.3 81.9 %all-to-all-start.4 = ((bf16[8,256,1792]{2,1,0:T(8,128)(2,1)}), bf16[8,256,1792]{2,1,0:T(8,128)(2,1)}, u32[]{:S(2)}, u32[]{:S(2)}) async-start(bf16[8,256,1792]{2,1,0:T(8,128)(2,1)} %param.12), calls=%async_computation.4 | async-start | bytes 14680064 | tf_op jit(solution)/shard_map/all_to_all | solution.py:86
  129.8 187.7 %all-gather.6.cloned.1.call-start = ((), (), s32[]{:S(2)}) async-start(), calls=%async_computation.12 | async-start | bytes 3096576 | tf_op jit(solution)/shard_map/all_gather | solution.py:11
  206.2 86.0 %all-to-all-start.2 = ((bf16[8,256,1792]{2,1,0:T(8,128)(2,1)}), bf16[8,256,1792]{2,1,0:T(8,128)(2,1)}, u32[]{:S(2)}, u32[]{:S(2)}) async-start(bf16[8,256,1792]{2,1,0:T(8,128)(2,1)} %param.13), calls=%async_computation.2 | async-start | bytes 14680064 | tf_op jit(solution)/shard_map/all_to_all | solution.py:87
  211.6 115.8 %all-gather.4.cloned.1.call-start = ((), (), s32[]{:S(2)}) async-start(), calls=%async_computation.11 | async-start | bytes 3096576 | tf_op jit(solution)/shard_map/all_gather | solution.py:12
  212.7 201.1 %all-reduce.4.cloned.1.call-start = ((), (), s32[]{:S(2)}) async-start(), calls=%async_computation.13 | async-start | bytes 5505024
  317.5 6.5 copy-start.2
  317.6 6.8 copy-start.3
  324.3 10.2 %slice-start = ((s8[7340032]{0:T(1024)(128)(4,1)}), s8[3145728]{0:T(1024)(128)(4,1)S(1)}, s32[]{:S(2)}) async-start(s8[7340032]{0:T(1024)(128)(4,1)} %bitcast.71), calls=%async_computation.14 | async-start | bytes 6291456
  327.4 7.1 slice-start.1
  327.4 8.4 %slice-start.2 = ((s8[7340032]{0:T(1024)(128)(4,1)}), s8[3145728]{0:T(1024)(128)(4,1)S(1)}, s32[]{:S(2)}) async-start(s8[7340032]{0:T(1024)(128)(4,1)} %bitcast.73), calls=%async_computation.16 | async-start | bytes 6291456
  334.5 2.2 slice-start.3
  338.0 4.4 copy-start.11
  338.0 81.7 %copy-start.5 = (bf16[2,96,7168]{2,0,1:T(2,128)(2,1)S(1)}, bf16[2,96,7168]{2,0,1:T(2,128)(2,1)}, u32[]{:S(2)}) copy-start(bf16[2,96,7168]{2,0,1:T(2,128)(2,1)} %all-gather.4.cloned.1.call-done) | copy-start | bytes 8257540
  338.0 81.7 %copy-start.6 = (bf16[2,96,256]{2,1,0:T(8,128)(2,1)S(1)}, bf16[2,96,256]{2,1,0:T(8,128)(2,1)}, u32[]{:S(2)}) copy-start(bf16[2,96,256]{2,1,0:T(8,128)(2,1)} %get-tuple-element.6) | copy-start | bytes 294916
  360.7 55.1 %all-to-all-start.7 = ((bf16[2,4,3]{2,0,1:T(2,128)(2,1)}), bf16[2,4,3]{2,0,1:T(2,128)(2,1)S(1)}, u32[]{:S(2)}, u32[]{:S(2)}) async-start(bf16[2,4,3]{2,0,1:T(2,128)(2,1)} %copy.114), calls=%async_computation.7 | async-start | bytes 4096 | tf_op jit(solution)/shard_map/all_to_all | solution.py:103
  415.8 27.8 %all-to-all-start.6 = ((bf16[2,12,7168]{2,0,1:T(2,128)(2,1)}), bf16[2,12,7168]{2,0,1:T(2,128)(2,1)S(1)}, u32[]{:S(2)}, u32[]{:S(2)}) async-start(bf16[2,12,7168]{2,0,1:T(2,128)(2,1)} %constant_dynamic-slice_fusion), calls=%async_computation.6 | async-start | bytes 688128 | tf_op jit(solution)/shard_map/all_to_all | solution.py:100
  443.5 5.7 copy-start.4
  443.5 85.6 %all-to-all-start.10 = ((bf16[2,256,7168]{1,0,2:T(2,128)(2,1)}), bf16[2,256,7168]{1,0,2:T(2,128)(2,1)}, u32[]{:S(2)}, u32[]{:S(2)}) async-start(bf16[2,256,7168]{1,0,2:T(2,128)(2,1)} %copy.122), calls=%async_computation.10 | async-start | bytes 14680064 | tf_op jit(solution)/shard_map/all_to_all | solution.py:110
  529.2 86.1 %all-to-all-start.8 = ((bf16[2,256,7168]{1,0,2:T(2,128)(2,1)}), bf16[2,256,7168]{1,0,2:T(2,128)(2,1)}, u32[]{:S(2)}, u32[]{:S(2)}) async-start(bf16[2,256,7168]{1,0,2:T(2,128)(2,1)} %copy.116), calls=%async_computation.8 | async-start | bytes 14680064 | tf_op jit(solution)/shard_map/all_to_all | solution.py:108
  558.5 62.3 %copy-start.10 = (s32[8,2]{0,1:T(2,128)S(1)}, s32[8,2]{0,1:T(2,128)}, u32[]{:S(2)}) copy-start(s32[8,2]{0,1:T(2,128)} %copy-done.9) | copy-start | bytes 196
  558.5 63.6 %copy-start.8 = (f32[24,8]{0,1:T(8,128)S(1)}, f32[24,8]{0,1:T(8,128)}, u32[]{:S(2)}) copy-start(f32[24,8]{0,1:T(8,128)} %copy-done.7) | copy-start | bytes 2308
  615.3 86.0 %all-to-all-start.9 = ((bf16[2,256,7168]{1,0,2:T(2,128)(2,1)}), bf16[2,256,7168]{1,0,2:T(2,128)(2,1)}, u32[]{:S(2)}, u32[]{:S(2)}) async-start(bf16[2,256,7168]{1,0,2:T(2,128)(2,1)} %copy.119), calls=%async_computation.9 | async-start | bytes 14680064 | tf_op jit(solution)/shard_map/all_to_all | solution.py:109
  701.3 18.5 %copy-start.1 = (bf16[8,7168]{1,0:T(8,128)(2,1)S(1)}, bf16[8,7168]{1,0:T(8,128)(2,1)}, u32[]{:S(2)}) copy-start(bf16[8,7168]{1,0:T(8,128)(2,1)} %param.7) | copy-start | bytes 344068
Sparse Core Ops, SparseCore 0:
  132.3 36.6 all-gather.5
  214.1 36.6 all-gather.3
  342.5 71.2 all-reduce.3
where the time goes:
time: 738 us; the launch traced here: 727 us
  waiting for transfers between devices  304 us (41%)
  local copies, waits for them, and re-layouts  203 us (28%)
  blocking collectives  123 us (17%)
  starting transfers between devices  43.4 us (6%)
  matrix products  38.2 us (5%)
  between operations  15.2 us (2%)
    all_to_all x1, blocking collectives, local(): lax.all_to_all(gate_weight, 'ep', split_axis=0, concat_axis=2, tiled=True)  85.4 us
    all_to_all x1, waiting for transfers between devices, local(): lax.all_to_all(up_weight, 'ep', split_axis=0, concat_axis=2, tiled=True)  75.3 us
    all_to_all x1, waiting for transfers between devices, local(): lax.all_to_all(grad_gate, 'ep', split_axis=2, concat_axis=0, tiled=True)  56.8 us
    all_to_all x1, waiting for transfers between devices, local(): lax.all_to_all(grad_down, 'ep', split_axis=2, concat_axis=0, tiled=True)  56.2 us
    unnamed x4, waiting for transfers between devices  49.9 us
    all_to_all x1, waiting for transfers between devices, local(): lax.all_to_all(grad_up, 'ep', split_axis=2, concat_axis=0, tiled=True)  41.4 us
    all_to_all x2, local copies, waits for them, and re-layouts, local(): lax.all_to_all(down_weight, 'ep', split_axis=0, concat_axis=2, tiled=True)  25.3 us
    all_to_all x2, local copies, waits for them, and re-layouts, local(): lax.all_to_all(gate_weight, 'ep', split_axis=0, concat_axis=2, tiled=True)  25.3 us
  transfers between devices with their start and end apart: 12, of which 8 were waited for; matrix products, arithmetic and copies ran while one was open for 23% of the time, Pallas kernels for 0%

commit v1 on v0

v1 whole, which is shorter than its diff:
```python
import jax
import jax.numpy as jnp
from jax import lax
from jax.sharding import PartitionSpec as P


def local(tokens, cotangent, routing, route_gates, gate_weight, up_weight, down_weight):
    rows, width = tokens.shape
    top = routing.shape[1]
    experts, units, part = gate_weight.shape
    ep, tp = lax.axis_size("ep"), lax.axis_size("tp")
    total = ep * tp * rows
    f32, bf16 = jnp.float32, jnp.bfloat16

    both = jnp.stack([tokens, cotangent]).reshape(2 * rows, width)
    both = lax.all_to_all(both, "ep", split_axis=1, concat_axis=0, tiled=True)
    both = lax.all_gather(both, "tp", axis=0, tiled=False).reshape(tp, ep, 2, rows, part)
    x = both[:, :, 0].reshape(total, part)
    dy = both[:, :, 1].reshape(total, part)
    routes = lax.all_gather(lax.all_gather(routing, "ep", axis=0), "tp", axis=0)
    mask = routes.reshape(total, top)[:, :, None] == jnp.arange(experts, dtype=jnp.int32)
    gates = lax.all_gather(route_gates, "tp", axis=0).astype(f32)

    wg = gate_weight.reshape(experts * units, part)
    wu = up_weight.reshape(experts * units, part)
    wd = down_weight.reshape(experts * units, part)

    def pre(a, w):
        full = lax.dot_general(a, w, (((1,), (1,)), ((), ())), preferred_element_type=f32)
        full = full.reshape(total, 1, experts, units)
        return jnp.sum(jnp.where(mask[..., None], full, 0.0), axis=2).astype(bf16)

    partial = jnp.stack([pre(x, wg), pre(x, wu), pre(dy, wd)])
    partial = partial.reshape(3, tp, ep, rows, top, units)
    partial = lax.all_to_all(partial, "ep", split_axis=2, concat_axis=0, tiled=True)
    sums = jnp.sum(partial.reshape(ep, 3, tp, rows, top, units).astype(f32), axis=0)
    gate, upper, reverse = sums[0], sums[1], sums[2]
    factor = gates[..., None]
    sigma = jax.nn.sigmoid(gate)
    silu = gate * sigma
    hidden = (silu * upper).astype(bf16).astype(f32)
    back = factor * reverse
    route_part = jnp.sum(hidden * reverse, axis=-1)
    d_gate = (back * upper * sigma * (1.0 + gate * (1.0 - sigma))).astype(bf16)
    d_up = (back * silu).astype(bf16)
    scaled = (factor * hidden).astype(bf16)
    route_grad = lax.psum_scatter(route_part, "tp", scatter_dimension=0, tiled=False)

    acts = jnp.stack([d_gate, d_up, scaled])
    acts = lax.all_gather(acts, "ep", axis=2).reshape(3, total, top, 1, units)

    def spread(a):
        wide = jnp.where(mask[..., None], a, jnp.zeros((), bf16))
        return jnp.sum(wide, axis=1, dtype=bf16).reshape(total, experts * units)

    dg, du, sc = spread(acts[0]), spread(acts[1]), spread(acts[2])
    dx = jnp.dot(dg, wg, preferred_element_type=f32) + jnp.dot(du, wu, preferred_element_type=f32)
    dx = dx.astype(bf16).reshape(tp, ep, rows, part)
    dx = lax.psum_scatter(dx, "tp", scatter_dimension=0, tiled=False)
    token_grad = lax.all_to_all(dx, "ep", split_axis=0, concat_axis=2, tiled=True).reshape(rows, width)

    def weight(a, b):
        out = lax.dot_general(a, b, (((0,), (0,)), ((), ())), preferred_element_type=f32)
        return out.astype(bf16).reshape(experts, units, part)

    return token_grad, route_grad, weight(dg, x), weight(du, x), weight(sc, dy)


def solution(mesh):
    row, mat = P(("ep", "tp"), None), P(None, "tp", "ep")
    return jax.shard_map(
        local,
        mesh=mesh,
        in_specs=(row, row, row, row, mat, mat, mat),
        out_specs=(row, row, mat, mat, mat),
        check_vma=False,
    )
```

time: 738 us -> 171 us (0.23); the launches traced: 727 us -> 170 us
  waiting for transfers between devices: 304 us -> 9.55 us
  local copies, waits for them, and re-layouts: 203 us -> 17.3 us
  blocking collectives: 123 us -> 74.4 us
  starting transfers between devices: 43.4 us -> 7.12 us
  other arithmetic: 0.39 us -> 11.2 us
    all_to_all x9 -> x2, waiting for transfers between devices: 254 us -> 4.84 us  [the longest x1 3.77 us: local(): lax.all_to_all(dx, 'ep', split_axis=0, concat_axis=2, tiled=True)]
    all_to_all x17 -> x2, local copies, waits for them, and re-layouts: 135 us -> 0.19 us  [local(): both = lax.all_to_all(both, 'ep', split_axis=1, concat_axis=0, tiled=True)]
    all_to_all x2 -> x1, blocking collectives: 94.9 us -> 10.7 us  [local(): both = lax.all_to_all(both, 'ep', split_axis=1, concat_axis=0, tiled=True)]
    convert_element_type x6 -> x4, local copies, waits for them, and re-layouts: 60.2 us -> 0.1 us  [the longest x3 0.09 us: pre(): return jnp.sum(jnp.where(mask[..., None], full, 0.0), axis=2).astype(bf16)]
    unnamed x4 -> x2, waiting for transfers between devices: 49.9 us -> 0.03 us
    all_gather x1 -> x4, blocking collectives: 11.9 us -> 49.5 us  [the longest x2 21.7 us: local(): routes = lax.all_gather(lax.all_gather(routing, 'ep', axis=0), 'tp', axis=0)]
    all_to_all x9 -> x2, starting transfers between devices: 43.3 us -> 7.08 us  [the longest x1 3.62 us: local(): lax.all_to_all(partial, 'ep', split_axis=2, concat_axis=0, tiled=True)]
    reduce_sum x2 -> x4, other arithmetic: 0.26 us -> 9.66 us  [the longest x1 5.2 us: pre(): return jnp.sum(jnp.where(mask[..., None], full, 0.0), axis=2).astype(bf16)]
  transfers between devices with their start and end apart: 12 -> 4, of which waited for: 8 -> 3; matrix products, arithmetic and copies ran while one was open for 23% -> 12% of each run, Pallas kernels for 0% -> 0%
where the time goes in v1:
time: 171 us; the launch traced here: 170 us
  blocking collectives  74.4 us (44%)
  matrix products  36.3 us (21%)
  local copies, waits for them, and re-layouts  17.3 us (10%)
  between operations  14.4 us (8%)
  other arithmetic  11.2 us (7%)
  waiting for transfers between devices  9.55 us (6%)
  starting transfers between devices  7.12 us (4%)
    all_gather x2, blocking collectives, local(): routes = lax.all_gather(lax.all_gather(routing, 'ep', axis=0), 'tp', axis=0)  21.7 us
    all_gather x1, blocking collectives, local(): acts = lax.all_gather(acts, 'ep', axis=2).reshape(3, total, top, 1, units)  17.5 us
    dot_general x3, matrix products, weight(): lax.dot_general(a, b, (((0,), (0,)), ((), ())), preferred_element_type=f32)  15.4 us
    unnamed x1, blocking collectives  14.2 us
    all_to_all x1, blocking collectives, local(): both = lax.all_to_all(both, 'ep', split_axis=1, concat_axis=0, tiled=True)  10.7 us
    all_gather x1, blocking collectives, local(): gates = lax.all_gather(route_gates, 'tp', axis=0).astype(f32)  10.3 us
    dot_general x3, matrix products, pre(): lax.dot_general(a, w, (((1,), (1,)), ((), ())), preferred_element_type=f32)  9.48 us
    dot_general x1, matrix products, local(): jnp.dot(dg, wg, preferred_element_type=f32)  6.2 us
  transfers between devices with their start and end apart: 4, of which 3 were waited for; matrix products, arithmetic and copies ran while one was open for 12% of the time, Pallas kernels for 0%

profile of v1, /device:TPU:0, one launch (start us, length us, event | category | flops | bytes accessed | tf_op | source)
XLA Modules:
  0.0 170.2 jit_solution(18122071795983895160)
XLA Ops:
  7.2 0.0 all-gather.8.cloned.1.call-start
  7.2 1.0 pad_maximum_fusion.1
  8.2 0.2 all_to_all.30
  8.4 10.7 %all_to_all.40 = bf16[16,4,1792]{2,0,1:T(8,128)(2,1)} all-to-all(bf16[16,4,1792]{2,0,1:T(8,128)(2,1)S(1)} %copy.111), channel_id=1, replica_groups=mesh['ep'=4,'tp'=8] {'ep'}, dimensions={1} | all-to-all | bytes 458752 | tf_op jit(solution)/shard_map/all_to_all | solution.py:16
  19.1 0.0 all-gather.8.cloned.1.call-update
  19.1 7.4 %all-gather.4 = s32[4,8,2]{1,2,0:T(2,128)S(1)} all-gather(s32[1,8,2]{1,2,0:T(2,128)} %bitcast.118), channel_id=2, replica_groups=mesh['ep'=4,'tp'=8] {'ep'}, dimensions={0}, use_global_device_ids=true | all-gather | bytes 320 | tf_op jit(solution)/shard_map/all_gather | solution.py:20
  26.5 14.3 %all-gather.1 = s32[32,8,2]{1,2,0:T(2,128)S(1)} all-gather(s32[4,8,2]{1,2,0:T(2,128)S(1)} %all-gather.4), channel_id=3, replica_groups=mesh['ep'=4,'tp'=8] {'tp'}, dimensions={0}, use_global_device_ids=true | all-gather | bytes 2304 | tf_op jit(solution)/shard_map/all_gather | solution.py:20
  40.8 0.3 copy.132
  41.1 0.3 iota_compare_fusion
  41.4 4.7 %all-gather.8.cloned.1.call-done = bf16[8,64,1792]{2,1,0:T(8,128)(2,1)} async-done(((bf16[1,64,1792]{2,1,0:T(8,128)(2,1)}), bf16[8,64,1792]{2,1,0:T(8,128)(2,1)}) %all-gather.8.cloned.1.call-update) | async-done | bytes 1835024 | tf_op jit(solution)/shard_map/all_gather | solution.py:17
  46.1 0.0 slice-start.2
  46.1 1.7 %fusion.8 = (bf16[8,4,1,8,1792]{4,3,2,1,0:T(8,128)(2,1)S(1)}, bf16[8,4,1,8,1792]{4,3,2,1,0:T(8,128)(2,1)S(1)}) fusion(bf16[8,4,2,8,1792]{4,3,2,1,0:T(8,128)(2,1)} %bitcast.105), kind=kLoop, calls=%fused_computation.36 | loop fusion | bytes 3670016 | tf_op jit(solution)/shard_map/slice | solution.py:19
  47.8 0.0 copy-start.1
  47.8 0.9 copy-done.1
  48.8 5.3 %fusion.13 = f32[256,8,256]{2,0,1:T(8,128)S(1)} fusion(bf16[256,1792,1]{1,0,2:T(8,128)(2,1)S(1)} %bitcast.102, bf16[8,256,1792]{2,1,0:T(8,128)(2,1)} %param.13), kind=kOutput, calls=%fused_computation.41 | convolution fusion | flops 1879048192 | bytes 10354688 | tf_op jit(solution)/shard_map/dot_general | solution.py:29
  54.1 0.0 slice-start
  54.1 1.2 copy.116
  55.3 0.0 slice-done.2
  55.4 0.0 slice-done.3
  55.4 0.0 slice-start.1
  55.4 2.1 %fusion.12 = f32[256,8,256]{2,0,1:T(8,128)S(1)} fusion(bf16[256,1792,1]{1,0,2:T(8,128)(2,1)S(1)} %bitcast.94, bf16[8,256,1792]{2,1,0:T(8,128)(2,1)S(1)} %bitcast.99), kind=kOutput, calls=%fused_computation.40 | convolution fusion | flops 1879048192 | bytes 10354688 | tf_op jit(solution)/shard_map/dot_general | solution.py:29
  57.5 1.2 copy.114
  58.7 0.0 slice-done
  58.7 0.0 slice-done.1
  58.7 2.1 %fusion.11 = f32[256,8,256]{2,0,1:T(8,128)S(1)} fusion(bf16[256,1792,1]{1,0,2:T(8,128)(2,1)S(1)} %bitcast.95, bf16[8,256,1792]{2,1,0:T(8,128)(2,1)S(1)} %bitcast.93), kind=kOutput, calls=%fused_computation.39 | convolution fusion | flops 1879048192 | bytes 10354688 | tf_op jit(solution)/shard_map/dot_general | solution.py:29
  60.8 1.2 copy.112
  62.0 5.2 %select_reduce_fusion.2 = (bf16[256,2,256]{2,1,0:T(2,128)(2,1)S(1)}, bf16[256,2,256]{2,1,0:T(2,128)(2,1)S(1)}, bf16[256,2,256]{2,1,0:T(2,128)(2,1)S(1)}) fusion(f32[256,8,256]{2,1,0:T(8,128)S(1)} %copy.112, pred[256,2,8]{2,1,0:T(4,128)(4,1)S(1)} %iota_compare_fusion, f32[256,8,256]{2,1,0:T(8,128)S(1)} %copy.114, f32[256,8,256]{2,1,0:T(8,128)S(1)} %copy.116), kind=kLoop, calls=%fused_computation.5 | loop fusion | flops 5898240 | bytes 7081984 | tf_op jit(solution)/shard_map/reduce_sum | solution.py:31
  67.3 0.0 copy-start.3
  67.4 0.1 pad_maximum_fusion
  67.5 2.0 %copy.118 = bf16[3,8,4,8,2,256]{5,4,3,1,0,2:T(2,128)(2,1)} copy(bf16[3,8,4,8,2,256]{5,3,2,1,4,0:T(8,128)(2,1)S(1)} %pad_maximum_fusion) | data formatting | bytes 1572864 | tf_op jit(solution)/shard_map/stack | solution.py:33
  69.4 3.6 %all-to-all-start.1 = ((bf16[3,8,4,8,2,256]{5,4,3,1,0,2:T(2,128)(2,1)}), bf16[3,8,4,8,2,256]{5,4,3,1,0,2:T(2,128)(2,1)S(1)}, u32[]{:S(2)}, u32[]{:S(2)}) async-start(bf16[3,8,4,8,2,256]{5,4,3,1,0,2:T(2,128)(2,1)} %copy.118), calls=%async_computation.1 | async-start | bytes 1572864 | tf_op jit(solution)/shard_map/all_to_all | solution.py:35
  73.1 0.0 reduce-scatter.2.cloned.1.call-start
  73.1 0.0 copy-done.3
  73.1 10.3 %all-gather.5 = bf16[8,8,2]{1,2,0:T(2,128)(2,1)S(1)} all-gather(bf16[1,8,2]{1,2,0:T(2,128)(2,1)S(1)} %bitcast.119), channel_id=4, replica_groups=mesh['ep'=4,'tp'=8] {'tp'}, dimensions={0}, use_global_device_ids=true | all-gather | bytes 288 | tf_op jit(solution)/shard_map/all_gather | solution.py:22
  83.3 1.1 all-to-all-done.1
  84.4 0.8 convert_reduce_fusion
  85.2 0.1 fusion.10
  85.3 0.1 multiply_convert_fusion.3
  85.5 17.5 %all-gather.3 = bf16[3,8,32,2,256]{4,2,3,1,0:T(8,128)(2,1)S(1)} all-gather(bf16[3,8,8,2,256]{4,2,3,1,0:T(8,128)(2,1)S(1)} %pad_maximum_fusion.2), channel_id=5, replica_groups=mesh['ep'=4,'tp'=8] {'ep'}, dimensions={2}, use_global_device_ids=true | all-gather | bytes 983040 | tf_op jit(solution)/shard_map/all_gather | solution.py:50
  103.0 0.1 fusion.9
  103.1 0.3 copy.126
  103.4 0.3 copy.123
  103.7 0.3 copy.131
  104.0 3.5 %select_reduce_fusion.3 = (bf16[256,8,256]{2,1,0:T(8,128)(2,1)}, bf16[256,8,256]{2,1,0:T(8,128)(2,1)S(1)}, bf16[256,8,256]{2,1,0:T(8,128)(2,1)}) fusion(pred[256,2,8]{2,1,0:T(4,128)(4,1)S(1)} %iota_compare_fusion, bf16[256,2,256]{2,1,0:T(2,128)(2,1)S(1)} %copy.131, bf16[256,2,256]{2,1,0:T(2,128)(2,1)S(1)} %copy.123, bf16[256,2,256]{2,1,0:T(2,128)(2,1)S(1)} %copy.126), kind=kLoop, calls=%fused_computation.10 | loop fusion | flops 4718592 | bytes 3936256 | tf_op jit(solution)/shard_map/reduce_sum | solution.py:54
  107.5 0.8 copy.128
  108.3 1.6 copy.129
  110.0 5.2 %convolution_bitcast_fusion = f32[256,1792]{1,0:T(8,128)S(1)} fusion(bf16[256,8,256]{0,2,1:T(8,128)(2,1)S(1)} %copy.129, bf16[8,256,1792]{2,1,0:T(8,128)(2,1)} %param.12), kind=kOutput, calls=%fused_computation.6 | convolution fusion | flops 1879048192 | bytes 10223616 | tf_op jit(solution)/shard_map/dot_general | solution.py:57
  115.2 0.0 copy-start.4
  115.2 6.2 %fusion.1 = bf16[256,1792]{1,0:T(8,128)(2,1)} fusion(f32[256,1792]{1,0:T(8,128)S(1)} %convolution_bitcast_fusion, bf16[256,8,256]{0,2,1:T(8,128)(2,1)S(1)} %copy.128, bf16[8,256,1792]{2,1,0:T(8,128)(2,1)} %param.11), kind=kOutput, calls=%fused_computation.9 | convolution fusion | flops 1879965696 | bytes 11141120 | tf_op jit(solution)/shard_map/dot_general | solution.py:57
  121.4 0.0 reduce-scatter.2.cloned.1.call-update
  121.4 0.0 copy-done.4
  121.4 0.6 dynamic-slice
  122.0 2.5 %copy.137 = bf16[32,8,8,256]{3,1,2,0:T(8,128)(2,1)} copy(bf16[32,8,8,256]{3,2,1,0:T(8,128)(2,1)} %bitcast.101) | data formatting | bytes 2097152
  124.5 0.1 fusion.2
  124.7 14.2 %all-reduce = f32[8,8,2]{1,2,0:T(2,128)S(1)} all-reduce(f32[8,8,2]{1,2,0:T(2,128)S(1)} %fusion.2), channel_id=7, replica_groups=mesh['ep'=4,'tp'=8] {'tp'}, use_global_device_ids=true, to_apply=%region_8.9.clone | all-reduce | flops 128 | bytes 1024
  138.8 5.1 %convolution_convert_fusion.1 = bf16[2048,1792]{1,0:T(8,128)(2,1)} fusion(bf16[256,2048]{0,1:T(8,128)(2,1)S(1)} %bitcast.91, bf16[256,1792]{1,0:T(8,128)(2,1)S(1)} %bitcast.96), kind=kOutput, calls=%fused_computation.1 | convolution fusion | flops 1882718208 | bytes 9306112 | tf_op jit(solution)/shard_map/dot_general | solution.py:63
  144.0 5.1 %convolution_convert_fusion.2 = bf16[2048,1792]{1,0:T(8,128)(2,1)} fusion(bf16[256,2048]{0,1:T(8,128)(2,1)S(1)} %bitcast.90, bf16[256,1792]{1,0:T(8,128)(2,1)S(1)} %bitcast.97), kind=kOutput, calls=%fused_computation.2 | convolution fusion | flops 1882718208 | bytes 9306112 | tf_op jit(solution)/shard_map/dot_general | solution.py:63
  149.1 0.0 copy-done
  149.1 0.0 copy-done.2
  149.1 5.2 %convolution_convert_fusion = bf16[2048,1792]{1,0:T(8,128)(2,1)} fusion(bf16[256,2048]{1,0:T(8,128)(2,1)S(1)} %bitcast.100, bf16[256,1792]{1,0:T(8,128)(2,1)S(1)} %bitcast.103), kind=kOutput, calls=%fused_computation | convolution fusion | flops 1882718208 | bytes 9306112 | tf_op jit(solution)/shard_map/dot_general | solution.py:63
  154.3 3.5 %all-to-all-start.2 = ((bf16[4,8,1792]{2,1,0:T(8,128)(2,1)}), bf16[4,8,1792]{2,1,0:T(8,128)(2,1)S(1)}, u32[]{:S(2)}, u32[]{:S(2)}) async-start(bf16[4,8,1792]{2,1,0:T(8,128)(2,1)} %bitcast.117), calls=%async_computation.3 | async-start | bytes 229376 | tf_op jit(solution)/shard_map/all_to_all | solution.py:60
  157.7 1.2 dynamic-slice_bitcast_fusion
  159.0 3.8 %all-to-all-done.2 = bf16[4,8,1792]{2,1,0:T(8,128)(2,1)S(1)} async-done(((bf16[4,8,1792]{2,1,0:T(8,128)(2,1)}), bf16[4,8,1792]{2,1,0:T(8,128)(2,1)S(1)}, u32[]{:S(2)}, u32[]{:S(2)}) %all-to-all-start.2) | async-done | bytes 114720 | tf_op jit(solution)/shard_map/all_to_all | solution.py:60
  162.7 0.6 copy.162
  (16 shorter events, 0.2 us)
Async XLA Ops:
  7.2 38.9 %all-gather.8.cloned.1.call-start = ((), (), s32[]{:S(2)}) async-start(), calls=%async_computation.4 | async-start | bytes 2064384 | tf_op jit(solution)/shard_map/all_gather | solution.py:17
  46.1 9.2 %slice-start.2 = ((s8[7340032]{0:T(1024)(128)(4,1)}), s8[4194304]{0:T(1024)(128)(4,1)S(1)}, s32[]{:S(2)}) async-start(s8[7340032]{0:T(1024)(128)(4,1)} %bitcast.98), calls=%async_computation.8 | async-start | bytes 8388608
  47.8 1.0 copy-start.1
  48.8 6.6 %slice-start.3 = ((s8[7340032]{0:T(1024)(128)(4,1)}), s8[3145728]{0:T(1024)(128)(4,1)S(1)}, s32[]{:S(2)}) async-start(s8[7340032]{0:T(1024)(128)(4,1)} %bitcast.98), calls=%async_computation.9 | async-start | bytes 6291456
  54.1 4.6 %slice-start = ((s8[7340032]{0:T(1024)(128)(4,1)}), s8[4194304]{0:T(1024)(128)(4,1)S(1)}, s32[]{:S(2)}) async-start(s8[7340032]{0:T(1024)(128)(4,1)} %bitcast.92), calls=%async_computation.6 | async-start | bytes 8388608
  55.4 3.3 %slice-start.1 = ((s8[7340032]{0:T(1024)(128)(4,1)}), s8[3145728]{0:T(1024)(128)(4,1)S(1)}, s32[]{:S(2)}) async-start(s8[7340032]{0:T(1024)(128)(4,1)} %bitcast.92), calls=%async_computation.7 | async-start | bytes 6291456
  67.3 5.8 %copy-start.3 = (bf16[8,2]{0,1:T(2,128)(2,1)S(1)}, bf16[8,2]{0,1:T(2,128)(2,1)}, u32[]{:S(2)}) copy-start(bf16[8,2]{0,1:T(2,128)(2,1)} %param.10) | copy-start | bytes 100
  69.4 15.0 %all-to-all-start.1 = ((bf16[3,8,4,8,2,256]{5,4,3,1,0,2:T(2,128)(2,1)}), bf16[3,8,4,8,2,256]{5,4,3,1,0,2:T(2,128)(2,1)S(1)}, u32[]{:S(2)}, u32[]{:S(2)}) async-start(bf16[3,8,4,8,2,256]{5,4,3,1,0,2:T(2,128)(2,1)} %copy.118), calls=%async_computation.1 | async-start | bytes 1572864 | tf_op jit(solution)/shard_map/all_to_all | solution.py:35
  73.1 81.2 %reduce-scatter.2.cloned.1.call-start = ((), (), s32[]{:S(2)}) async-start(), calls=%async_computation.5 | async-start | bytes 1032192 | tf_op jit(solution)/shard_map/reduce_scatter | solution.py:59
  115.2 6.2 %copy-start.4 = (u32[32]{0:T(128)S(1)}, u32[32]{0:T(128)}, u32[]{:S(2)}) copy-start(u32[32]{0:T(128)} %constant.12) | copy-start | bytes 388
  144.0 5.1 %copy-start = (bf16[32,8,8,256]{3,1,2,0:T(8,128)(2,1)S(1)}, bf16[32,8,8,256]{3,1,2,0:T(8,128)(2,1)}, u32[]{:S(2)}) copy-start(bf16[32,8,8,256]{3,1,2,0:T(8,128)(2,1)} %copy.137) | copy-start | bytes 3145732
  144.0 5.1 %copy-start.2 = (bf16[8,4,1,8,1792]{4,3,2,1,0:T(8,128)(2,1)S(1)}, bf16[8,4,1,8,1792]{4,3,2,1,0:T(8,128)(2,1)}, u32[]{:S(2)}) copy-start(bf16[8,4,1,8,1792]{4,3,2,1,0:T(8,128)(2,1)} %copy-done.1) | copy-start | bytes 2752516
  154.3 8.4 %all-to-all-start.2 = ((bf16[4,8,1792]{2,1,0:T(8,128)(2,1)}), bf16[4,8,1792]{2,1,0:T(8,128)(2,1)S(1)}, u32[]{:S(2)}, u32[]{:S(2)}) async-start(bf16[4,8,1792]{2,1,0:T(8,128)(2,1)} %bitcast.117), calls=%async_computation.3 | async-start | bytes 229376 | tf_op jit(solution)/shard_map/all_to_all | solution.py:60
Sparse Core Ops, SparseCore 0:
  19.2 26.8 all-gather.7
  121.5 29.8 reduce-scatter.1

commit v2 on v1

v2 whole, which is shorter than its diff:
```python
import functools

import jax
import jax.numpy as jnp
from jax import lax
from jax.experimental import pallas as pl
from jax.experimental.pallas import tpu as pltpu
from jax.sharding import PartitionSpec as P

F32, BF16 = jnp.float32, jnp.bfloat16
LANES = 128
VMEM_BYTES = 58 * 1024 * 1024


def main_kernel(
    ep, tp, rows, top,
    src_ref, wg_hbm, wu_hbm, wd_hbm,
    x_ref, y_ref, dg_ref, du_ref, sc_ref, dx_ref, route_ref,
    wg, wu, wd, xy, meta, pick, sel, rcv, acts, acc, rp, rr,
    w_sem, p1_send, p2_send, p3_send, xy_recv, sel_send, sel_recv, act_send, act_recv, rt_send, rt_recv,
):
    me_e, me_t = lax.axis_index("ep"), lax.axis_index("tp")
    experts, units, part = wg.shape
    total = ep * tp * rows
    block = tp * rows
    half = tp // 2
    sibling = me_t + 1 - 2 * lax.rem(me_t, 2)

    def dev(e, t):
        return {"ep": e, "tp": t}

    def remote(src, dst, s_sem, r_sem, e, t):
        return pltpu.make_async_remote_copy(
            src_ref=src, dst_ref=dst, send_sem=s_sem, recv_sem=r_sem,
            device_id=dev(e, t), device_id_type=pl.DeviceIdType.MESH,
        )

    loads = [
        pltpu.make_async_copy(h, v, w_sem.at[i])
        for i, (h, v) in enumerate(((wg_hbm, wg), (wu_hbm, wu), (wd_hbm, wd)))
    ]
    for c in loads:
        c.start()

    barrier = pltpu.get_barrier_semaphore()
    for d in range(1, ep):
        pl.semaphore_signal(
            barrier, inc=1, device_id=dev(lax.rem(me_e + d, ep), me_t), device_id_type=pl.DeviceIdType.MESH
        )
    for d in range(1, tp):
        pl.semaphore_signal(
            barrier, inc=1, device_id=dev(me_e, lax.rem(me_t + d, tp)), device_id_type=pl.DeviceIdType.MESH
        )
    pl.semaphore_wait(barrier, ep - 1 + tp - 1)

    sends = []

    def go(c):
        c.start()
        sends.append(c)

    for d in range(1, ep):
        q = lax.rem(me_e + d, ep)
        go(remote(src_ref.at[q], xy.at[me_e, me_t], p1_send.at[d - 1], xy_recv.at[me_e, me_t], q, me_t))
    xy[me_e, me_t] = src_ref[me_e]

    def landed(s, t):
        remote(xy.at[s, t], xy.at[s, t], p1_send.at[0], xy_recv.at[s, t], me_e, sibling).wait_recv()

    for d in range(ep):
        s = lax.rem(me_e + d, ep)
        if d:
            landed(s, me_t)
        for j in range(half - 1, 0, -1):
            t = lax.rem(me_t + 2 * j, tp)
            go(remote(xy.at[s, me_t], xy.at[s, me_t], p2_send.at[d, j], xy_recv.at[s, me_t], me_e, t))
        go(remote(xy.at[s, me_t], xy.at[s, me_t], p2_send.at[d, 0], xy_recv.at[s, me_t], me_e, sibling))
    for d in range(ep):
        s = lax.rem(me_e + d, ep)
        for j in range(1, half):
            t = lax.rem(me_t + 2 * j, tp)
            landed(s, t)
            go(remote(xy.at[s, t], xy.at[s, t], p3_send.at[d, j - 1], xy_recv.at[s, t], me_e, sibling))
    for d in range(ep):
        s = lax.rem(me_e + d, ep)
        for j in range(half):
            landed(s, lax.rem(sibling + 2 * j, tp))

    def split(s, carry):
        both = xy[s].astype(F32)
        first = pl.multiple_of(s * block, block)
        left = both[:, :rows, :].reshape(block, part + LANES)
        x_ref[pl.ds(first, block), :] = left[:, :part].astype(BF16)
        meta[pl.ds(first, block), :] = left[:, part:]
        y_ref[pl.ds(first, block), :] = both[:, rows:, :part].reshape(block, part).astype(BF16)
        return carry

    lax.fori_loop(0, ep, split, 0)
    for k in range(top):
        pick[k] = jnp.broadcast_to(meta[:, k : k + 1], (total, units))

    for m, (a_ref, w) in enumerate(((x_ref, wg), (x_ref, wu), (y_ref, wd))):
        loads[m].wait()

        def expert(e, carry, a_ref=a_ref, w=w):
            full = lax.dot_general(a_ref[...], w[e], (((1,), (1,)), ((), ())), preferred_element_type=F32)
            here = e.astype(F32)
            for k in range(top):
                acc[k] = jnp.where(pick[k] == here, full, acc[k])
            return carry

        acc[...] = jnp.zeros_like(acc)
        lax.fori_loop(0, experts, expert, 0)
        for k in range(top):
            sel[m, :, k * block : (k + 1) * block, :] = acc[k].astype(BF16).reshape(ep, block, units)
        for d in range(1, ep):
            q = lax.rem(me_e + d, ep)
            go(remote(sel.at[m, q], rcv.at[m, me_e], sel_send.at[m, d - 1], sel_recv.at[m, me_e], q, me_t))

    sums = []
    for m in range(3):
        value = sel[m, me_e].astype(F32)
        for d in range(1, ep):
            s = lax.rem(me_e + d, ep)
            remote(rcv.at[m, s], rcv.at[m, s], p1_send.at[0], sel_recv.at[m, s], s, me_t).wait_recv()
            value = value + rcv[m, s].astype(F32)
        sums.append(value)
    gate, upper, reverse = sums
    mine = meta[pl.ds(pl.multiple_of(me_e * block, block), block), :]
    factor = jnp.concatenate([mine[:, top + k : top + k + 1] for k in range(top)], axis=0)
    sigma = jax.nn.sigmoid(gate)
    silu = gate * sigma
    hidden = (silu * upper).astype(BF16).astype(F32)
    back = factor * reverse
    acts[0, me_e] = (back * upper * sigma * (1.0 + gate * (1.0 - sigma))).astype(BF16)
    acts[1, me_e] = (back * silu).astype(BF16)
    acts[2, me_e] = (factor * hidden).astype(BF16)
    for a in range(3):
        for d in range(1, ep):
            q = lax.rem(me_e + d, ep)
            go(remote(acts.at[a, me_e], acts.at[a, me_e], act_send.at[a, d - 1], act_recv.at[a, me_e], q, me_t))
    term = jnp.sum(hidden * reverse, axis=1, keepdims=True)
    term = jnp.broadcast_to(term, (top * block, LANES))
    for k in range(top):
        rp[:, k] = term[k * block : (k + 1) * block].reshape(tp, rows, LANES)
    for d in range(1, tp):
        t = lax.rem(me_t + d, tp)
        go(remote(rp.at[t], rr.at[me_t], rt_send.at[d - 1], rt_recv.at[me_t], me_e, t))

    for a, out in enumerate((dg_ref, du_ref, sc_ref)):
        for d in range(1, ep):
            s = lax.rem(me_e + d, ep)
            remote(acts.at[a, s], acts.at[a, s], p1_send.at[0], act_recv.at[a, s], s, me_t).wait_recv()
        for k in range(top):
            acc[k] = acts[a, :, k * block : (k + 1) * block, :].reshape(total, units).astype(F32)

        def spread(e, carry, out=out):
            here = e.astype(F32)
            value = jnp.zeros((total, units), F32)
            for k in range(top):
                value = jnp.where(pick[k] == here, acc[k], value)
            out[e] = value.astype(BF16)
            return carry

        lax.fori_loop(0, experts, spread, 0)

    def columns(c, carry):
        at = pl.ds(pl.multiple_of(c * 256, 256), 256)
        value = jnp.zeros((total, 256), F32)
        for e in range(experts):
            value = value + jnp.dot(dg_ref[e], wg[e, :, at], preferred_element_type=F32)
            value = value + jnp.dot(du_ref[e], wu[e, :, at], preferred_element_type=F32)
        dx_ref[:, at] = value.astype(BF16)
        return carry

    lax.fori_loop(0, part // 256, columns, 0)

    value = rp[me_t]
    for d in range(1, tp):
        t = lax.rem(me_t + d, tp)
        remote(rr.at[t], rr.at[t], p1_send.at[0], rt_recv.at[t], me_e, t).wait_recv()
        value = value + rr[t]
    route_ref[...] = value
    for c in sends:
        c.wait_send()


def grad_kernel(dg, du, sc, x, y, gg, ug, wdg):
    for a, b, out in ((dg, x, gg), (du, x, ug), (sc, y, wdg)):
        out[0] = lax.dot_general(
            a[0], b[...], (((0,), (0,)), ((), ())), preferred_element_type=F32
        ).astype(BF16)


def local(tokens, cotangent, routing, route_gates, gate_weight, up_weight, down_weight):
    rows, width = tokens.shape
    top = routing.shape[1]
    experts, units, part = gate_weight.shape
    ep, tp = lax.axis_size("ep"), lax.axis_size("tp")
    total, block, half = ep * tp * rows, tp * rows, tp // 2
    wide = part + LANES

    note = jnp.concatenate([routing.astype(BF16), route_gates], axis=1)
    note = jnp.pad(note, ((0, rows), (0, LANES - 2 * top)))
    both = jnp.concatenate([tokens, cotangent], axis=0).reshape(2 * rows, ep, part).transpose(1, 0, 2)
    src = jnp.concatenate([both, jnp.broadcast_to(note, (ep, 2 * rows, LANES))], axis=2)

    vmem, hbm = pl.BlockSpec(memory_space=pltpu.VMEM), pl.BlockSpec(memory_space=pl.ANY)
    dma = pltpu.SemaphoreType.DMA
    dense = jax.ShapeDtypeStruct((experts, total, units), BF16)
    flat = jax.ShapeDtypeStruct((total, part), BF16)
    x, y, dg, du, sc, dx, route = pl.pallas_call(
        functools.partial(main_kernel, ep, tp, rows, top),
        out_shape=(flat, flat, dense, dense, dense, flat, jax.ShapeDtypeStruct((top, rows, LANES), F32)),
        in_specs=[vmem, hbm, hbm, hbm],
        out_specs=(vmem,) * 7,
        scratch_shapes=[
            pltpu.VMEM((experts, units, part), BF16),
            pltpu.VMEM((experts, units, part), BF16),
            pltpu.VMEM((experts, units, part), BF16),
            pltpu.VMEM((ep, tp, 2 * rows, wide), BF16),
            pltpu.VMEM((total, LANES), F32),
            pltpu.VMEM((top, total, units), F32),
            pltpu.VMEM((3, ep, top * block, units), BF16),
            pltpu.VMEM((3, ep, top * block, units), BF16),
            pltpu.VMEM((3, ep, top * block, units), BF16),
            pltpu.VMEM((top, total, units), F32),
            pltpu.VMEM((tp, top, rows, LANES), F32),
            pltpu.VMEM((tp, top, rows, LANES), F32),
            dma((3,)),
            dma((ep - 1,)),
            dma((ep, half)),
            dma((ep, half)),
            dma((ep, tp)),
            dma((3, ep)),
            dma((3, ep)),
            dma((3, ep)),
            dma((3, ep)),
            dma((tp,)),
            dma((tp,)),
        ],
        compiler_params=pltpu.CompilerParams(
            collective_id=0, has_side_effects=True, vmem_limit_bytes=VMEM_BYTES
        ),
        name="main",
    )(src, gate_weight, up_weight, down_weight)

    dx = lax.psum_scatter(dx.reshape(ep, tp, rows, part), "tp", scatter_dimension=1, tiled=False)

    strip = pl.BlockSpec((1, total, units), lambda e: (e, 0, 0))
    whole = pl.BlockSpec((total, part), lambda e: (0, 0))
    slab = pl.BlockSpec((1, units, part), lambda e: (e, 0, 0))
    grad = jax.ShapeDtypeStruct((experts, units, part), BF16)
    gate_grad, up_grad, down_grad = pl.pallas_call(
        grad_kernel,
        grid=(experts,),
        out_shape=(grad, grad, grad),
        in_specs=[strip, strip, strip, whole, whole],
        out_specs=(slab, slab, slab),
        compiler_params=pltpu.CompilerParams(vmem_limit_bytes=VMEM_BYTES // 2),
        cost_estimate=pl.CostEstimate(
            flops=6 * experts * total * units * part,
            bytes_accessed=6 * experts * units * (part + total) + 4 * total * part,
            transcendentals=0,
        ),
        name="grads",
    )(dg, du, sc, x, y)

    token_grad = lax.all_to_all(dx, "ep", split_axis=0, concat_axis=2, tiled=True).reshape(rows, width)
    return token_grad, route[:, :, 0].T, gate_grad, up_grad, down_grad


def solution(mesh):
    row, mat = P(("ep", "tp"), None), P(None, "tp", "ep")
    return jax.shard_map(
        local,
        mesh=mesh,
        in_specs=(row, row, row, row, mat, mat, mat),
        out_specs=(row, row, mat, mat, mat),
        check_vma=False,
    )
```

time: 171 us -> 152 us (0.89)
  Pallas kernels: 0 us -> 76.5 us
  blocking collectives: 74.4 us -> 0 us
  matrix products: 36.3 us -> 0 us
  waiting for transfers between devices: 9.55 us -> 44.2 us
  other arithmetic: 11.2 us -> 3.03 us
  local copies, waits for them, and re-layouts: 17.3 us -> 10.3 us
  starting transfers between devices: 7.12 us -> 3.51 us
    pallas_call x0 -> x2, Pallas kernels: none -> 76.5 us  [the longest x1 66.7 us: local(): pl.pallas_call(functools.partial(main_kernel, ep, tp, rows, top), out_sha...]
    all_gather x4 -> x0, blocking collectives: 49.5 us -> none  [the longest x2 21.7 us: local(): routes = lax.all_gather(lax.all_gather(routing, 'ep', axis=0), 'tp', axis=0)]
    unnamed x2, waiting for transfers between devices: 0.03 us -> 39.9 us
    dot_general x8 -> x0, matrix products: 36.3 us -> none  [the longest x3 15.4 us: weight(): lax.dot_general(a, b, (((0,), (0,)), ((), ())), preferred_element_type=f32)]
    unnamed x1 -> x0, blocking collectives: 14.2 us -> none
    all_to_all x1 -> x0, blocking collectives: 10.7 us -> none  [local(): both = lax.all_to_all(both, 'ep', split_axis=1, concat_axis=0, tiled=True)]
    reduce_sum x4 -> x0, other arithmetic: 9.66 us -> none  [the longest x1 5.2 us: pre(): return jnp.sum(jnp.where(mask[..., None], full, 0.0), axis=2).astype(bf16)]
    all_gather x1 -> x0, waiting for transfers between devices: 4.67 us -> none  [local(): lax.all_gather(both, 'tp', axis=0, tiled=False)]
  transfers between devices with their start and end apart: 4 -> 2, of which waited for: 3 -> 2; matrix products, arithmetic and copies ran while one was open for 12% -> 1% of each run, Pallas kernels for 0% -> 6%
where the time goes in v2:
time: 152 us
  Pallas kernels  76.5 us (50%)
  waiting for transfers between devices  44.2 us (29%)
  between operations  14.1 us (9%)
  local copies, waits for them, and re-layouts  10.3 us (7%)
  starting transfers between devices  3.51 us (2%)
  other arithmetic  3.03 us (2%)
    pallas_call x1, Pallas kernels, local(): pl.pallas_call(functools.partial(main_kernel, ep, tp, rows, top), out_sha...  66.7 us
    unnamed x2, waiting for transfers between devices  39.9 us
    pallas_call x1, Pallas kernels, local(): pl.pallas_call(grad_kernel, grid=(experts,), out_shape=(grad, grad, grad)...  9.8 us
    unnamed x17, local copies, waits for them, and re-layouts  7.38 us
    all_to_all x1, waiting for transfers between devices, local(): lax.all_to_all(dx, 'ep', split_axis=0, concat_axis=2, tiled=True)  4.33 us
    all_to_all x1, starting transfers between devices, local(): lax.all_to_all(dx, 'ep', split_axis=0, concat_axis=2, tiled=True)  3.47 us
  transfers between devices with their start and end apart: 2, of which 2 were waited for; matrix products, arithmetic and copies ran while one was open for 1% of the time, Pallas kernels for 6%

profile of v2, /device:TPU:0, one launch (start us, length us, event | category | flops | bytes accessed | tf_op | source)
XLA Modules:
  0.0 151.6 jit_solution(2797518767287948418)
XLA Ops:
  7.2 0.0 all-reduce.4.cloned.1.call-start
  7.2 0.7 convert_element_type.5
  7.9 0.7 pad_maximum_fusion.2
  8.6 0.1 copy.19
  8.7 1.0 pad_maximum_fusion.1
  9.7 0.7 pad_maximum_fusion.src_ref
  10.4 0.0 copy-start.6
  10.4 66.7 %main.1 = (bf16[256,1792]{1,0:T(8,128)(2,1)}, bf16[256,1792]{1,0:T(8,128)(2,1)}, bf16[8,256,256]{2,1,0:T(8,128)(2,1)}, bf16[8,256,256]{2,1,0:T(8,128)(2,1)}, bf1...) custom-call(bf16[4,16,1920]{2,1,0:T(8,128)(2,1)} %pad_maximum_fusion.src_ref, ...), custom_call_target="tpu_custom_call" | custom-call | tf_op jit(solution)/shard_map/main/pallas_call | solution.py:212
  77.1 0.0 all-reduce.4.cloned.1.call-update
  77.2 0.0 copy-done.6
  77.2 0.6 dynamic-slice
  77.8 0.0 copy-start
  77.8 1.2 copy-done
  79.0 0.0 copy-start.1
  79.0 1.2 copy-done.1
  80.2 0.0 copy-start.2
  80.2 1.2 copy-done.2
  81.5 0.0 copy-start.3
  81.5 1.2 copy-done.3
  82.6 0.0 copy-start.4
  82.6 1.2 copy-done.4
  83.8 0.0 copy-start.5
  83.8 9.8 %grads.1 = (bf16[8,256,1792]{2,1,0:T(8,128)(2,1)}, bf16[8,256,1792]{2,1,0:T(8,128)(2,1)}, bf16[8,256,1792]{2,1,0:T(8,128)(2,1)}) custom-call(bf16[8,256,256]{2,1,0:T(8,128)(2,1)S(1)} %copy-done, bf16[8,256,256]{2,1,0:T(8,128)(2,1)S(1)} %copy-done.1, bf16[8,256,256]{2,1,0:T(8,128)(2,1)S(1)} %copy-done.2, bf16[256,1792]{1,0:T(8,128)(2,1)S(1)} %copy-done.3, ...), custom_call_target="tpu_custom_call" | custom-call | flops 5637144576 | bytes 27000832 | tf_op jit(solution)/shard_map/grads/pallas_call | solution.py:254
  93.6 39.8 %all-reduce.4.cloned.1.call-done = bf16[4,8,8,1792]{3,2,1,0:T(8,128)(2,1)} async-done(((bf16[4,8,8,1792]{3,2,1,0:T(8,128)(2,1)}), bf16[4,8,8,1792]{3,2,1,0:T(8,128)(2,1)}) %all-reduce.4.cloned.1.call-update) | async-done | bytes 917520
  133.5 2.2 %dynamic-slice_bitcast_fusion = bf16[4,8,1792]{2,1,0:T(8,128)(2,1)} fusion(bf16[4,8,8,1792]{3,2,1,0:T(8,128)(2,1)} %all-reduce.4.cloned.1.call-done, u32[]{:T(128)} %bitcast.4), kind=kLoop, calls=%fused_computation.3 | loop fusion | bytes 229380 | tf_op jit(solution)/shard_map/reduce_scatter | solution.py:248
  135.7 3.5 %all-to-all-start = ((bf16[4,8,1792]{2,1,0:T(8,128)(2,1)}), bf16[4,8,1792]{2,1,0:T(8,128)(2,1)S(1)}, u32[]{:S(2)}, u32[]{:S(2)}) async-start(bf16[4,8,1792]{2,1,0:T(8,128)(2,1)} %dynamic-slice_bitcast_fusion), calls=%async_computation | async-start | bytes 229376 | tf_op jit(solution)/shard_map/all_to_all | solution.py:269
  139.1 0.0 copy-done.5
  139.1 0.6 slice_reduce_fusion
  139.8 4.3 %all-to-all-done = bf16[4,8,1792]{2,1,0:T(8,128)(2,1)S(1)} async-done(((bf16[4,8,1792]{2,1,0:T(8,128)(2,1)}), bf16[4,8,1792]{2,1,0:T(8,128)(2,1)S(1)}, u32[]{:S(2)}, u32[]{:S(2)}) %all-to-all-start) | async-done | bytes 114720 | tf_op jit(solution)/shard_map/all_to_all | solution.py:269
  144.1 0.6 copy.25
  (3 shorter events, 0.0 us)
Async XLA Ops:
  7.2 126.3 %all-reduce.4.cloned.1.call-start = ((), (), s32[]{:S(2)}) async-start(), calls=%async_computation.1 | async-start | bytes 1835008
  10.4 66.8 %copy-start.6 = (u32[32]{0:T(128)S(1)}, u32[32]{0:T(128)}, u32[]{:S(2)}) copy-start(u32[32]{0:T(128)} %constant.11) | copy-start | bytes 388
  77.8 1.2 copy-start
  79.0 1.2 copy-start.1
  80.2 1.2 copy-start.2
  81.5 1.2 copy-start.3
  82.6 1.2 copy-start.4
  83.8 55.3 %copy-start.5 = (f32[2,8,128]{2,1,0:T(8,128)S(1)}, f32[2,8,128]{2,1,0:T(8,128)}, u32[]{:S(2)}) copy-start(f32[2,8,128]{2,1,0:T(8,128)} %get-tuple-element.16) | copy-start | bytes 24580
  135.7 8.5 %all-to-all-start = ((bf16[4,8,1792]{2,1,0:T(8,128)(2,1)}), bf16[4,8,1792]{2,1,0:T(8,128)(2,1)S(1)}, u32[]{:S(2)}, u32[]{:S(2)}) async-start(bf16[4,8,1792]{2,1,0:T(8,128)(2,1)} %dynamic-slice_bitcast_fusion), calls=%async_computation | async-start | bytes 229376 | tf_op jit(solution)/shard_map/all_to_all | solution.py:269
Sparse Core Ops, SparseCore 0:
  77.3 56.1 all-reduce.3

commit v3 on v2

--- a/solution.py
+++ b/solution.py
@@ -14,10 +14,11 @@
 
 def main_kernel(
     ep, tp, rows, top,
-    src_ref, wg_hbm, wu_hbm, wd_hbm,
-    x_ref, y_ref, dg_ref, du_ref, sc_ref, dx_ref, route_ref,
-    wg, wu, wd, xy, meta, pick, sel, rcv, acts, acc, rp, rr,
+    tok_ref, cot_ref, note_ref, wg_hbm, wu_hbm, wd_hbm,
+    x_ref, y_ref, dg_ref, du_ref, sc_ref, grad_ref, route_ref,
+    wg, wu, wd, src_ref, xy, meta, pick, sel, rcv, acts, acc, rp, rr,
     w_sem, p1_send, p2_send, p3_send, xy_recv, sel_send, sel_recv, act_send, act_recv, rt_send, rt_recv,
+    pieces, sib, pair_sum, got, fin, home, a_send, a_recv, b_send, b_recv, c_send, c_recv,
 ):
     me_e, me_t = lax.axis_index("ep"), lax.axis_index("tp")
     experts, units, part = wg.shape
@@ -51,6 +52,12 @@
         pl.semaphore_signal(
             barrier, inc=1, device_id=dev(me_e, lax.rem(me_t + d, tp)), device_id_type=pl.DeviceIdType.MESH
         )
+    note = jnp.concatenate([note_ref[...], jnp.zeros_like(note_ref)], axis=0).astype(BF16)
+    for q in range(ep):
+        at = slice(q * part, (q + 1) * part)
+        both = jnp.concatenate([tok_ref[:, at].astype(F32), cot_ref[:, at].astype(F32)], axis=0)
+        src_ref[q, :, :part] = both.astype(BF16)
+        src_ref[q, :, part:] = note
     pl.semaphore_wait(barrier, ep - 1 + tp - 1)
 
     sends = []
@@ -147,14 +154,14 @@
         t = lax.rem(me_t + d, tp)
         go(remote(rp.at[t], rr.at[me_t], rt_send.at[d - 1], rt_recv.at[me_t], me_e, t))
 
-    for a, out in enumerate((dg_ref, du_ref, sc_ref)):
+    def spread_out(a, out):
         for d in range(1, ep):
             s = lax.rem(me_e + d, ep)
             remote(acts.at[a, s], acts.at[a, s], p1_send.at[0], act_recv.at[a, s], s, me_t).wait_recv()
         for k in range(top):
             acc[k] = acts[a, :, k * block : (k + 1) * block, :].reshape(total, units).astype(F32)
 
-        def spread(e, carry, out=out):
+        def spread(e, carry):
             here = e.astype(F32)
             value = jnp.zeros((total, units), F32)
             for k in range(top):
@@ -164,16 +171,63 @@
 
         lax.fori_loop(0, experts, spread, 0)
 
-    def columns(c, carry):
-        at = pl.ds(pl.multiple_of(c * 256, 256), 256)
-        value = jnp.zeros((total, 256), F32)
+    spread_out(0, dg_ref)
+    spread_out(1, du_ref)
+
+    chunks, span = pieces.shape[0], pieces.shape[-1]
+    core = lax.rem(me_t, 2)
+    pair = me_t // 2
+
+    def to_core(c):
+        return remote(pieces.at[c, 1 - core], sib.at[c], a_send.at[c], a_recv.at[c], me_e, sibling)
+
+    def to_pair(c, j):
+        t = lax.rem(me_t + 2 * j, tp)
+        return remote(pair_sum.at[c, t // 2], got.at[c, pair], b_send.at[c, j - 1], b_recv.at[c, pair], me_e, t)
+
+    def compute(c):
+        at = pl.ds(pl.multiple_of(c * span, span), span)
+        value = jnp.zeros((total, span), F32)
         for e in range(experts):
             value = value + jnp.dot(dg_ref[e], wg[e, :, at], preferred_element_type=F32)
             value = value + jnp.dot(du_ref[e], wu[e, :, at], preferred_element_type=F32)
-        dx_ref[:, at] = value.astype(BF16)
+        value = value.reshape(ep, tp, rows, span)
+        for t in range(tp):
+            pieces[c, t % 2, t // 2] = value[:, t].reshape(ep * rows, span).astype(BF16)
+        to_core(c).start()
+
+    def relay(c):
+        to_core(c).wait_recv()
+        pair_sum[c] = (pieces[c, core].astype(F32) + sib[c].astype(F32)).astype(BF16)
+        for j in range(1, half):
+            to_pair(c, j).start()
+
+    def step(c, carry):
+        compute(c)
+        relay(c - 1)
         return carry
 
-    lax.fori_loop(0, part // 256, columns, 0)
+    compute(0)
+    lax.fori_loop(1, chunks, step, 0)
+    relay(chunks - 1)
+
+    spread_out(2, sc_ref)
+
+    def collect(c, carry):
+        value = pair_sum[c, pair].astype(F32)
+        for j in range(1, half):
+            p = lax.rem(pair + j, half)
+            remote(got.at[c, p], got.at[c, p], a_send.at[0], b_recv.at[c, p], me_e, sibling).wait_recv()
+            value = value + got[c, p].astype(F32)
+        at = pl.ds(pl.multiple_of(c * span, span), span)
+        fin[:, :, at] = value.reshape(ep, rows, span)
+        return carry
+
+    lax.fori_loop(0, chunks, collect, 0)
+    for d in range(1, ep):
+        q = lax.rem(me_e + d, ep)
+        go(remote(fin.at[q], home.at[me_e], c_send.at[d - 1], c_recv.at[me_e], q, me_t))
+    home[me_e] = fin[me_e]
 
     value = rp[me_t]
     for d in range(1, tp):
@@ -181,6 +235,19 @@
         remote(rr.at[t], rr.at[t], p1_send.at[0], rt_recv.at[t], me_e, t).wait_recv()
         value = value + rr[t]
     route_ref[...] = value
+    for d in range(1, ep):
+        s = lax.rem(me_e + d, ep)
+        remote(home.at[s], home.at[s], p1_send.at[0], c_recv.at[s], s, me_t).wait_recv()
+    for s in range(ep):
+        grad_ref[:, s * part : (s + 1) * part] = home[s].astype(BF16)
+
+    def drain(c, carry):
+        to_core(c).wait_send()
+        for j in range(1, half):
+            to_pair(c, j).wait_send()
+        return carry
+
+    lax.fori_loop(0, chunks, drain, 0)
     for c in sends:
         c.wait_send()
 
@@ -200,24 +267,25 @@
     total, block, half = ep * tp * rows, tp * rows, tp // 2
     wide = part + LANES
 
-    note = jnp.concatenate([routing.astype(BF16), route_gates], axis=1)
-    note = jnp.pad(note, ((0, rows), (0, LANES - 2 * top)))
-    both = jnp.concatenate([tokens, cotangent], axis=0).reshape(2 * rows, ep, part).transpose(1, 0, 2)
-    src = jnp.concatenate([both, jnp.broadcast_to(note, (ep, 2 * rows, LANES))], axis=2)
+    span = 256 if part % 256 == 0 else LANES
+    chunks = part // span
+    note = jnp.concatenate([routing.astype(F32), route_gates.astype(F32)], axis=1)
+    note = jnp.pad(note, ((0, 0), (0, LANES - 2 * top)))
 
     vmem, hbm = pl.BlockSpec(memory_space=pltpu.VMEM), pl.BlockSpec(memory_space=pl.ANY)
     dma = pltpu.SemaphoreType.DMA
     dense = jax.ShapeDtypeStruct((experts, total, units), BF16)
     flat = jax.ShapeDtypeStruct((total, part), BF16)
-    x, y, dg, du, sc, dx, route = pl.pallas_call(
+    x, y, dg, du, sc, token_grad, route = pl.pallas_call(
         functools.partial(main_kernel, ep, tp, rows, top),
-        out_shape=(flat, flat, dense, dense, dense, flat, jax.ShapeDtypeStruct((top, rows, LANES), F32)),
-        in_specs=[vmem, hbm, hbm, hbm],
+        out_shape=(flat, flat, dense, dense, dense, jax.ShapeDtypeStruct((rows, width), BF16), jax.ShapeDtypeStruct((top, rows, LANES), F32)),
+        in_specs=[vmem, vmem, vmem, hbm, hbm, hbm],
         out_specs=(vmem,) * 7,
         scratch_shapes=[
             pltpu.VMEM((experts, units, part), BF16),
             pltpu.VMEM((experts, units, part), BF16),
             pltpu.VMEM((experts, units, part), BF16),
+            pltpu.VMEM((ep, 2 * rows, wide), BF16),
             pltpu.VMEM((ep, tp, 2 * rows, wide), BF16),
             pltpu.VMEM((total, LANES), F32),
             pltpu.VMEM((top, total, units), F32),
@@ -238,14 +306,24 @@
             dma((3, ep)),
             dma((tp,)),
             dma((tp,)),
+            pltpu.VMEM((chunks, 2, half, ep * rows, span), BF16),
+            pltpu.VMEM((chunks, half, ep * rows, span), BF16),
+            pltpu.VMEM((chunks, half, ep * rows, span), BF16),
+            pltpu.VMEM((chunks, half, ep * rows, span), BF16),
+            pltpu.VMEM((ep, rows, part), F32),
+            pltpu.VMEM((ep, rows, part), F32),
+            dma((chunks,)),
+            dma((chunks,)),
+            dma((chunks, half)),
+            dma((chunks, half)),
+            dma((ep,)),
+            dma((ep,)),
         ],
         compiler_params=pltpu.CompilerParams(
             collective_id=0, has_side_effects=True, vmem_limit_bytes=VMEM_BYTES
         ),
         name="main",
-    )(src, gate_weight, up_weight, down_weight)
-
-    dx = lax.psum_scatter(dx.reshape(ep, tp, rows, part), "tp", scatter_dimension=1, tiled=False)
+    )(tokens, cotangent, note, gate_weight, up_weight, down_weight)
 
     strip = pl.BlockSpec((1, total, units), lambda e: (e, 0, 0))
     whole = pl.BlockSpec((total, part), lambda e: (0, 0))
@@ -257,7 +335,7 @@
         out_shape=(grad, grad, grad),
         in_specs=[strip, strip, strip, whole, whole],
         out_specs=(slab, slab, slab),
-        compiler_params=pltpu.CompilerParams(vmem_limit_bytes=VMEM_BYTES // 2),
+        compiler_params=pltpu.CompilerParams(vmem_limit_bytes=VMEM_BYTES),
         cost_estimate=pl.CostEstimate(
             flops=6 * experts * total * units * part,
             bytes_accessed=6 * experts * units * (part + total) + 4 * total * part,
@@ -266,7 +344,6 @@
         name="grads",
     )(dg, du, sc, x, y)
 
-    token_grad = lax.all_to_all(dx, "ep", split_axis=0, concat_axis=2, tiled=True).reshape(rows, width)
     return token_grad, route[:, :, 0].T, gate_grad, up_grad, down_grad
 
 

time: 152 us -> 94.9 us (0.62)
  waiting for transfers between devices: 44.2 us -> 0 us
  between operations: 14.1 us -> 0.64 us
  Pallas kernels: 76.5 us -> 89.7 us
  local copies, waits for them, and re-layouts: 10.3 us -> 3.49 us
  starting transfers between devices: 3.51 us -> 0 us
  other arithmetic: 3.03 us -> 0.68 us
    unnamed x2 -> x0, waiting for transfers between devices: 39.9 us -> none
    pallas_call x1, Pallas kernels: 66.7 us -> 77.9 us  [local(): pl.pallas_call(functools.partial(main_kernel, ep, tp, rows, top), out_sha...]
    unnamed x17 -> x5, local copies, waits for them, and re-layouts: 7.38 us -> 2.15 us
    all_to_all x1 -> x0, waiting for transfers between devices: 4.33 us -> none  [local(): lax.all_to_all(dx, 'ep', split_axis=0, concat_axis=2, tiled=True)]
    all_to_all x1 -> x0, starting transfers between devices: 3.47 us -> none  [local(): lax.all_to_all(dx, 'ep', split_axis=0, concat_axis=2, tiled=True)]
    reduce_scatter x1 -> x0, local copies, waits for them, and re-layouts: 2.2 us -> none  [local(): lax.psum_scatter(dx.reshape(ep, tp, rows, part), 'tp', scatter_dimension=...]
    pallas_call x1, Pallas kernels: 9.8 us -> 11.9 us  [local(): pl.pallas_call(grad_kernel, grid=(experts,), out_shape=(grad, grad, grad)...]
    concatenate x3 -> x1, other arithmetic: 2.34 us -> 0.67 us  [local(): jnp.concatenate([routing.astype(F32), route_gates.astype(F32)], axis=1)]
  transfers between devices with their start and end apart: 2 -> 0, of which waited for: 2 -> 0; matrix products, arithmetic and copies ran while one was open for 1% -> 0% of each run, Pallas kernels for 6% -> 0%
where the time goes in v3:
time: 94.9 us; the launch traced here: 94.5 us
  Pallas kernels  89.7 us (95%)
  local copies, waits for them, and re-layouts  3.49 us (4%)
    pallas_call x1, Pallas kernels, local(): pl.pallas_call(functools.partial(main_kernel, ep, tp, rows, top), out_sha...  77.9 us
    pallas_call x1, Pallas kernels, local(): pl.pallas_call(grad_kernel, grid=(experts,), out_shape=(grad, grad, grad)...  11.9 us
    unnamed x5, local copies, waits for them, and re-layouts  2.15 us

profile of v3, /device:TPU:0, one launch (start us, length us, event | category | flops | bytes accessed | tf_op | source)
XLA Modules:
  0.0 94.5 jit_solution(17921511336114510126)
XLA Ops:
  0.6 0.7 copy.15
  1.4 0.8 copy.14
  2.1 0.7 select_maximum_fusion.note_ref
  2.8 77.9 %main.1 = (bf16[256,1792]{1,0:T(8,128)(2,1)}, bf16[256,1792]{1,0:T(8,128)(2,1)}, bf16[8,256,256]{2,1,0:T(8,128)(2,1)}, bf16[8,256,256]{2,1,0:T(8,128)(2,1)}, bf1...) custom-call(bf16[8,7168]{1,0:T(8,128)(2,1)} %tok_ref.1, bf16[8,7168]{1,0:T(8,128)(2,1)} %cot_ref.1, ...), custom_call_target="tpu_custom_call" | custom-call | tf_op jit(solution)/shard_map/main/pallas_call | solution.py:279
  80.7 1.3 %slice_reduce_fusion = f32[2,8]{1,0:T(2,128)} fusion(f32[2,8,128]{2,1,0:T(8,128)} %get-tuple-element.16), kind=kLoop, calls=%fused_computation | loop fusion | bytes 128 | tf_op jit(solution)/shard_map/slice | solution.py:347
  82.0 0.0 copy-start
  82.0 11.9 %grads.1 = (bf16[8,256,1792]{2,1,0:T(8,128)(2,1)}, bf16[8,256,1792]{2,1,0:T(8,128)(2,1)}, bf16[8,256,1792]{2,1,0:T(8,128)(2,1)}) custom-call(bf16[8,256,256]{2,1,0:T(8,128)(2,1)} %get-tuple-element.17.dg, bf16[8,256,256]{2,1,0:T(8,128)(2,1)} %get-tuple-element.18.du, bf16[8,256,256]{2,1,0:T(8,128)(2,1)} %get-tuple-element.19.sc, ...), custom_call_target="tpu_custom_call" | custom-call | flops 5637144576 | bytes 27000832 | tf_op jit(solution)/shard_map/grads/pallas_call | solution.py:332
  93.9 0.0 copy-done
  93.9 0.6 copy.17
  (2 shorter events, 0.0 us)
Async XLA Ops:
  82.0 11.9 %copy-start = (bf16[8,7168]{1,0:T(8,128)(2,1)S(1)}, bf16[8,7168]{1,0:T(8,128)(2,1)}, u32[]{:S(2)}) copy-start(bf16[8,7168]{1,0:T(8,128)(2,1)} %get-tuple-element.30) | copy-start | bytes 344068

commit v4 on v3

--- a/solution.py
+++ b/solution.py
@@ -53,11 +53,13 @@
             barrier, inc=1, device_id=dev(me_e, lax.rem(me_t + d, tp)), device_id_type=pl.DeviceIdType.MESH
         )
     note = jnp.concatenate([note_ref[...], jnp.zeros_like(note_ref)], axis=0).astype(BF16)
-    for q in range(ep):
-        at = slice(q * part, (q + 1) * part)
-        both = jnp.concatenate([tok_ref[:, at].astype(F32), cot_ref[:, at].astype(F32)], axis=0)
-        src_ref[q, :, :part] = both.astype(BF16)
-        src_ref[q, :, part:] = note
+    fold = part // 2
+    for i, ref in enumerate((tok_ref, cot_ref)):
+        for q in range(ep):
+            low, mid, high = q * part, q * part + fold, (q + 1) * part
+            both = jnp.concatenate([ref[:, low:mid].astype(F32), ref[:, mid:high].astype(F32)], axis=0)
+            src_ref[i, q, :, :fold] = both.astype(BF16)
+            src_ref[i, q, :, fold:] = note
     pl.semaphore_wait(barrier, ep - 1 + tp - 1)
 
     sends = []
@@ -66,58 +68,74 @@
         c.start()
         sends.append(c)
 
-    for d in range(1, ep):
-        q = lax.rem(me_e + d, ep)
-        go(remote(src_ref.at[q], xy.at[me_e, me_t], p1_send.at[d - 1], xy_recv.at[me_e, me_t], q, me_t))
-    xy[me_e, me_t] = src_ref[me_e]
-
-    def landed(s, t):
-        remote(xy.at[s, t], xy.at[s, t], p1_send.at[0], xy_recv.at[s, t], me_e, sibling).wait_recv()
-
-    for d in range(ep):
-        s = lax.rem(me_e + d, ep)
-        if d:
-            landed(s, me_t)
-        for j in range(half - 1, 0, -1):
-            t = lax.rem(me_t + 2 * j, tp)
-            go(remote(xy.at[s, me_t], xy.at[s, me_t], p2_send.at[d, j], xy_recv.at[s, me_t], me_e, t))
-        go(remote(xy.at[s, me_t], xy.at[s, me_t], p2_send.at[d, 0], xy_recv.at[s, me_t], me_e, sibling))
-    for d in range(ep):
-        s = lax.rem(me_e + d, ep)
-        for j in range(1, half):
-            t = lax.rem(me_t + 2 * j, tp)
-            landed(s, t)
-            go(remote(xy.at[s, t], xy.at[s, t], p3_send.at[d, j - 1], xy_recv.at[s, t], me_e, sibling))
-    for d in range(ep):
-        s = lax.rem(me_e + d, ep)
-        for j in range(half):
-            landed(s, lax.rem(sibling + 2 * j, tp))
-
-    def split(s, carry):
-        both = xy[s].astype(F32)
-        first = pl.multiple_of(s * block, block)
-        left = both[:, :rows, :].reshape(block, part + LANES)
-        x_ref[pl.ds(first, block), :] = left[:, :part].astype(BF16)
-        meta[pl.ds(first, block), :] = left[:, part:]
-        y_ref[pl.ds(first, block), :] = both[:, rows:, :part].reshape(block, part).astype(BF16)
-        return carry
-
-    lax.fori_loop(0, ep, split, 0)
+    for i in range(2):
+        for d in range(1, ep):
+            q = lax.rem(me_e + d, ep)
+            go(remote(
+                src_ref.at[i, q], xy.at[i, me_e, me_t], p1_send.at[i, d - 1], xy_recv.at[i, me_e, me_t], q, me_t
+            ))
+        xy[i, me_e, me_t] = src_ref[i, me_e]
+
+    def landed(i, s, t):
+        here = xy.at[i, s, t]
+        remote(here, here, p1_send.at[0, 0], xy_recv.at[i, s, t], me_e, sibling).wait_recv()
+
+    def along(i):
+        for d in range(ep):
+            s = lax.rem(me_e + d, ep)
+            if d:
+                landed(i, s, me_t)
+            here = xy.at[i, s, me_t]
+            for j in range(half - 1, 0, -1):
+                t = lax.rem(me_t + 2 * j, tp)
+                go(remote(here, here, p2_send.at[i, d, j], xy_recv.at[i, s, me_t], me_e, t))
+            go(remote(here, here, p2_send.at[i, d, 0], xy_recv.at[i, s, me_t], me_e, sibling))
+
+    def across(i):
+        for d in range(ep):
+            s = lax.rem(me_e + d, ep)
+            for j in range(1, half):
+                t = lax.rem(me_t + 2 * j, tp)
+                landed(i, s, t)
+                here = xy.at[i, s, t]
+                go(remote(here, here, p3_send.at[i, d, j - 1], xy_recv.at[i, s, t], me_e, sibling))
+
+    def unfold(i, out):
+        for d in range(ep):
+            s = lax.rem(me_e + d, ep)
+            for j in range(half):
+                landed(i, s, lax.rem(sibling + 2 * j, tp))
+
+        def split(s, carry):
+            both = xy[i, s].astype(F32)
+            at = pl.ds(pl.multiple_of(s * block, block), block)
+            left, right = both[:, :rows, :], both[:, rows:, :fold]
+            out[at, :fold] = left[:, :, :fold].reshape(block, fold).astype(BF16)
+            out[at, fold:] = right.reshape(block, fold).astype(BF16)
+            if i == 0:
+                meta[at, :] = left[:, :, fold:].reshape(block, LANES)
+            return carry
+
+        lax.fori_loop(0, ep, split, 0)
+
+    along(0)
+    along(1)
+    across(0)
+    unfold(0, x_ref)
     for k in range(top):
         pick[k] = jnp.broadcast_to(meta[:, k : k + 1], (total, units))
 
     for m, (a_ref, w) in enumerate(((x_ref, wg), (x_ref, wu), (y_ref, wd))):
         loads[m].wait()
 
-        def expert(e, carry, a_ref=a_ref, w=w):
+        if m == 1:
+            across(1)
+        if m == 2:
+            unfold(1, y_ref)
+        for e in range(experts):
             full = lax.dot_general(a_ref[...], w[e], (((1,), (1,)), ((), ())), preferred_element_type=F32)
-            here = e.astype(F32)
             for k in range(top):
-                acc[k] = jnp.where(pick[k] == here, full, acc[k])
-            return carry
-
-        acc[...] = jnp.zeros_like(acc)
-        lax.fori_loop(0, experts, expert, 0)
+                acc[k] = jnp.where(pick[k] == float(e), full, acc[k] if e else 0.0)
         for k in range(top):
             sel[m, :, k * block : (k + 1) * block, :] = acc[k].astype(BF16).reshape(ep, block, units)
         for d in range(1, ep):
@@ -129,7 +147,7 @@
         value = sel[m, me_e].astype(F32)
         for d in range(1, ep):
             s = lax.rem(me_e + d, ep)
-            remote(rcv.at[m, s], rcv.at[m, s], p1_send.at[0], sel_recv.at[m, s], s, me_t).wait_recv()
+            remote(rcv.at[m, s], rcv.at[m, s], p1_send.at[0, 0], sel_recv.at[m, s], s, me_t).wait_recv()
             value = value + rcv[m, s].astype(F32)
         sums.append(value)
     gate, upper, reverse = sums
@@ -157,7 +175,7 @@
     def spread_out(a, out):
         for d in range(1, ep):
             s = lax.rem(me_e + d, ep)
-            remote(acts.at[a, s], acts.at[a, s], p1_send.at[0], act_recv.at[a, s], s, me_t).wait_recv()
+            remote(acts.at[a, s], acts.at[a, s], p1_send.at[0, 0], act_recv.at[a, s], s, me_t).wait_recv()
         for k in range(top):
             acc[k] = acts[a, :, k * block : (k + 1) * block, :].reshape(total, units).astype(F32)
 
@@ -232,12 +250,13 @@
     value = rp[me_t]
     for d in range(1, tp):
         t = lax.rem(me_t + d, tp)
-        remote(rr.at[t], rr.at[t], p1_send.at[0], rt_recv.at[t], me_e, t).wait_recv()
+        remote(rr.at[t], rr.at[t], p1_send.at[0, 0], rt_recv.at[t], me_e, t).wait_recv()
         value = value + rr[t]
-    route_ref[...] = value
+    for k in range(top):
+        route_ref[:, k : k + 1] = value[k, :, :1]
     for d in range(1, ep):
         s = lax.rem(me_e + d, ep)
-        remote(home.at[s], home.at[s], p1_send.at[0], c_recv.at[s], s, me_t).wait_recv()
+        remote(home.at[s], home.at[s], p1_send.at[0, 0], c_recv.at[s], s, me_t).wait_recv()
     for s in range(ep):
         grad_ref[:, s * part : (s + 1) * part] = home[s].astype(BF16)
 
@@ -265,7 +284,7 @@
     experts, units, part = gate_weight.shape
     ep, tp = lax.axis_size("ep"), lax.axis_size("tp")
     total, block, half = ep * tp * rows, tp * rows, tp // 2
-    wide = part + LANES
+    wide = part // 2 + LANES
 
     span = 256 if part % 256 == 0 else LANES
     chunks = part // span
@@ -278,15 +297,15 @@
     flat = jax.ShapeDtypeStruct((total, part), BF16)
     x, y, dg, du, sc, token_grad, route = pl.pallas_call(
         functools.partial(main_kernel, ep, tp, rows, top),
-        out_shape=(flat, flat, dense, dense, dense, jax.ShapeDtypeStruct((rows, width), BF16), jax.ShapeDtypeStruct((top, rows, LANES), F32)),
+        out_shape=(flat, flat, dense, dense, dense, jax.ShapeDtypeStruct((rows, width), BF16), jax.ShapeDtypeStruct((rows, top), F32)),
         in_specs=[vmem, vmem, vmem, hbm, hbm, hbm],
         out_specs=(vmem,) * 7,
         scratch_shapes=[
             pltpu.VMEM((experts, units, part), BF16),
             pltpu.VMEM((experts, units, part), BF16),
             pltpu.VMEM((experts, units, part), BF16),
-            pltpu.VMEM((ep, 2 * rows, wide), BF16),
-            pltpu.VMEM((ep, tp, 2 * rows, wide), BF16),
+            pltpu.VMEM((2, ep, 2 * rows, wide), BF16),
+            pltpu.VMEM((2, ep, tp, 2 * rows, wide), BF16),
             pltpu.VMEM((total, LANES), F32),
             pltpu.VMEM((top, total, units), F32),
             pltpu.VMEM((3, ep, top * block, units), BF16),
@@ -296,10 +315,10 @@
             pltpu.VMEM((tp, top, rows, LANES), F32),
             pltpu.VMEM((tp, top, rows, LANES), F32),
             dma((3,)),
-            dma((ep - 1,)),
-            dma((ep, half)),
-            dma((ep, half)),
-            dma((ep, tp)),
+            dma((2, ep - 1)),
+            dma((2, ep, half)),
+            dma((2, ep, half)),
+            dma((2, ep, tp)),
             dma((3, ep)),
             dma((3, ep)),
             dma((3, ep)),
@@ -344,7 +363,7 @@
         name="grads",
     )(dg, du, sc, x, y)
 
-    return token_grad, route[:, :, 0].T, gate_grad, up_grad, down_grad
+    return token_grad, route, gate_grad, up_grad, down_grad
 
 
 def solution(mesh):

time: 94.9 us -> 89.8 us (0.946)
  Pallas kernels: 89.7 us -> 84.7 us
    pallas_call x1, Pallas kernels: 77.9 us -> 72.8 us  [local(): pl.pallas_call(functools.partial(main_kernel, ep, tp, rows, top), out_sha...]
    slice x1 -> x0, local copies, waits for them, and re-layouts: 1.35 us -> none  [local(): return (token_grad, route[:, :, 0].T, gate_grad, up_grad, down_grad)]
    unnamed x5 -> x6, local copies, waits for them, and re-layouts: 2.15 us -> 3.46 us
where the time goes in v4:
time: 89.8 us; the launch traced here: 89.5 us
  Pallas kernels  84.7 us (94%)
  local copies, waits for them, and re-layouts  3.46 us (4%)
    pallas_call x1, Pallas kernels, local(): pl.pallas_call(functools.partial(main_kernel, ep, tp, rows, top), out_sha...  72.8 us
    pallas_call x1, Pallas kernels, local(): pl.pallas_call(grad_kernel, grid=(experts,), out_shape=(grad, grad, grad)...  11.9 us
    unnamed x6, local copies, waits for them, and re-layouts  3.46 us

profile of v4, /device:TPU:0, one launch (start us, length us, event | category | flops | bytes accessed | tf_op | source)
XLA Modules:
  0.0 89.5 jit_solution(4059129486721663920)
XLA Ops:
  0.6 0.7 copy.13
  1.4 0.8 copy.12
  2.1 0.7 select_maximum_fusion.note_ref
  2.8 72.8 %main.1 = (bf16[256,1792]{1,0:T(8,128)(2,1)}, bf16[256,1792]{1,0:T(8,128)(2,1)}, bf16[8,256,256]{2,1,0:T(8,128)(2,1)}, bf16[8,256,256]{2,1,0:T(8,128)(2,1)}, bf1...) custom-call(bf16[8,7168]{1,0:T(8,128)(2,1)} %tok_ref.1, bf16[8,7168]{1,0:T(8,128)(2,1)} %cot_ref.1, ...), custom_call_target="tpu_custom_call" | custom-call | tf_op jit(solution)/shard_map/main/pallas_call | solution.py:298
  75.6 1.3 %copy.14 = f32[8,2]{0,1:T(2,128)} copy(f32[8,2]{1,0:T(8,128)} %get-tuple-element.26) | data formatting | bytes 128
  76.9 0.0 copy-start
  76.9 11.9 %grads.1 = (bf16[8,256,1792]{2,1,0:T(8,128)(2,1)}, bf16[8,256,1792]{2,1,0:T(8,128)(2,1)}, bf16[8,256,1792]{2,1,0:T(8,128)(2,1)}) custom-call(bf16[8,256,256]{2,1,0:T(8,128)(2,1)} %get-tuple-element.17.dg, bf16[8,256,256]{2,1,0:T(8,128)(2,1)} %get-tuple-element.18.du, bf16[8,256,256]{2,1,0:T(8,128)(2,1)} %get-tuple-element.19.sc, ...), custom_call_target="tpu_custom_call" | custom-call | flops 5637144576 | bytes 27000832 | tf_op jit(solution)/shard_map/grads/pallas_call | solution.py:351
  88.8 0.0 copy-done
  88.8 0.6 copy.16
  (2 shorter events, 0.0 us)
Async XLA Ops:
  76.9 11.9 %copy-start = (bf16[8,7168]{1,0:T(8,128)(2,1)S(1)}, bf16[8,7168]{1,0:T(8,128)(2,1)}, u32[]{:S(2)}) copy-start(bf16[8,7168]{1,0:T(8,128)(2,1)} %get-tuple-element.35) | copy-start | bytes 344068
